TPU v7x, 32 devices: a whole 2x2x4 slice. The times are simulated.
32 devices in a mesh: dp: 2 (over y), ctx: 4 (over x, core), exp: 4 (over z).
Axes of the slice: x: 2, y: 2, z: 4, core: 2. Of those that a mesh axis runs over, the one named last changes fastest.
Arguments:
- tokens: bfloat16 [2, 8, 1024, 1024], P(None, ('dp', 'exp'), 'ctx'), may hold values from -6 to 6
- routes: int32 [2, 8, 1024, 8], P(None, ('dp', 'exp'), 'ctx'), may hold values from 0 to 31, all different within a row
- cotangent: bfloat16 [2, 8, 1024, 1024], P(None, ('dp', 'exp'), 'ctx'), may hold values from -6 to 6
- norm_one: bfloat16 [1024], P(('dp', 'ctx')), may hold values from 0.5 to 1.5
- norm_two: bfloat16 [1024], P(('dp', 'ctx')), may hold values from 0.5 to 1.5
- w_query: bfloat16 [1024, 1024], P(('dp', 'ctx')), may hold values from -0.5 to 0.5
- w_key: bfloat16 [1024, 512], P(('dp', 'ctx')), may hold values from -0.5 to 0.5
- w_value: bfloat16 [1024, 512], P(('dp', 'ctx')), may hold values from -0.1875 to 0.1875
- w_out: bfloat16 [1024, 1024], P(('dp', 'ctx')), may hold values from -9.4375 to 9.4375
- w_router: bfloat16 [1024, 32], P(('dp', 'ctx')), may hold values from -0.09375 to 0.09375
- w_gate: bfloat16 [32, 1024, 512], P('exp', ('dp', 'ctx')), may hold values from -0.1875 to 0.1875
- w_up: bfloat16 [32, 1024, 512], P('exp', ('dp', 'ctx')), may hold values from -0.1875 to 0.1875
- w_down: bfloat16 [32, 512, 1024], P('exp', None, ('dp', 'ctx')), may hold values from -4.71875 to 4.71875
Outputs:
- layer_out: bfloat16 [2, 8, 1024, 1024], P(None, ('dp', 'exp'), 'ctx')
- input_grad: bfloat16 [2, 8, 1024, 1024], P(None, ('dp', 'exp'), 'ctx')
- norm_one_grad: float32 [1024], P(('dp', 'ctx'))
- norm_two_grad: float32 [1024], P(('dp', 'ctx'))
- query_grad: float32 [1024, 1024], P(('dp', 'ctx'))
- key_grad: float32 [1024, 512], P(('dp', 'ctx'))
- value_grad: float32 [1024, 512], P(('dp', 'ctx'))
- out_grad: float32 [1024, 1024], P(('dp', 'ctx'))
- router_grad: float32 [1024, 32], P(('dp', 'ctx'))
- gate_grad: float32 [32, 1024, 512], P('exp', ('dp', 'ctx'))
- up_grad: float32 [32, 1024, 512], P('exp', ('dp', 'ctx'))
- down_grad: float32 [32, 512, 1024], P('exp', None, ('dp', 'ctx'))
Inputs may be any that keep to these rules, and one draw needn't show every extreme that they name: `routes`: each token names 8 different experts.
All inputs are finite; a program needn't handle non-finite values.
Results may differ from a plain program's by a relative error of at most 0.024.
Values may be sent and summed in bfloat16 or wider, within the bound.
No kernel may reach another device: no remote copies, remote signals or barrier semaphores. Data moves between devices by JAX's collectives and lax.ppermute only.
A program may use at most 192 MiB of HBM per device.

v0:
```python
import jax
import jax.numpy as jnp
from jax import lax
from jax.sharding import PartitionSpec as P

H = 16
KVH = 8
HD = 64
EXPERTS = 32
FF = 512
TOPK = 8
BLOCK = 256
CAP = 72


EPSILON = 1e-06
BASE_THETA = 10000.0
NEGATIVE = -1e30
ATTENTION_MULT = 0.015625
RESIDUAL_MULT = 0.22


def rotation(offset, row_count, head_size):
    half_size = head_size // 2
    inverse = jnp.exp(
        jnp.arange(half_size, dtype=jnp.float32)
        * (-2.0 * jnp.log(jnp.float32(BASE_THETA)) / head_size)
    )
    places = (offset + jnp.arange(row_count, dtype=jnp.int32)).astype(jnp.float32)
    angles = places[:, None] * inverse[None, :]
    return (jnp.cos(angles), jnp.sin(angles))


def rotate(tensor, cosine, sine, forward):
    half_size = tensor.shape[-1] // 2
    former = tensor[..., :half_size]
    latter = tensor[..., half_size:]
    cosine = cosine[:, None, :]
    sine = sine[:, None, :] if forward else -sine[:, None, :]
    return jnp.concatenate([former * cosine - latter * sine, latter * cosine + former * sine], -1)


def normalize(values):
    factor = lax.rsqrt(jnp.mean(values * values, -1, keepdims=True) + EPSILON)
    return (values * factor, factor)


def piece_scores(query_grid, key_all, shard_at, row_count, query_ids):
    first_row = shard_at * row_count
    key_piece = lax.dynamic_slice_in_dim(key_all, first_row, row_count, 0).reshape(
        row_count, KVH, HD
    )
    raw_scores = (
        jnp.einsum("qkgd,tkd->kgqt", query_grid, key_piece, preferred_element_type=jnp.float32)
        * ATTENTION_MULT
    )
    key_ids = (first_row + jnp.arange(row_count, dtype=jnp.int32)) // BLOCK
    allowed = key_ids[None, :] <= query_ids[:, None]
    return (jnp.where(allowed, raw_scores, NEGATIVE), key_piece)


def value_slice(value_all, shard_at, row_count):
    return lax.dynamic_slice_in_dim(value_all, shard_at * row_count, row_count, 0).reshape(
        row_count, KVH, HD
    )


def fetch(norm_one, norm_two, w_query, w_key, w_value, w_out, w_router, w_gate, w_up, w_down):
    attention_set = (
        lax.all_gather(norm_one, ("dp", "ctx"), axis=0, tiled=True),
        lax.all_gather(norm_two, ("dp", "ctx"), axis=0, tiled=True),
        lax.all_gather(w_query, ("dp", "ctx"), axis=0, tiled=True),
        lax.all_gather(w_key, ("dp", "ctx"), axis=0, tiled=True),
        lax.all_gather(w_value, ("dp", "ctx"), axis=0, tiled=True),
        lax.all_gather(w_out, ("dp", "ctx"), axis=0, tiled=True),
        lax.all_gather(w_router, ("dp", "ctx"), axis=0, tiled=True),
    )
    expert_set = (
        lax.all_gather(w_gate, ("dp", "ctx"), axis=1, tiled=True),
        lax.all_gather(w_up, ("dp", "ctx"), axis=1, tiled=True),
        lax.all_gather(w_down, ("dp", "ctx"), axis=2, tiled=True),
    )
    return tuple(attention_set) + tuple(expert_set)


def on_device(
    tokens,
    routes,
    cotangent,
    norm_one,
    norm_two,
    w_query,
    w_key,
    w_value,
    w_out,
    w_router,
    w_gate,
    w_up,
    w_down,
):
    micro_count = tokens.shape[0]
    row_count = tokens.shape[2]
    model_width = tokens.shape[3]
    local_experts = w_gate.shape[0]
    group_size = H // KVH
    expert_slots = EXPERTS * CAP
    score_scale = ATTENTION_MULT
    ctx_count = lax.axis_size("ctx")
    ctx_index = lax.axis_index("ctx")
    cosine, sine = rotation(ctx_index * row_count, row_count, HD)
    query_ids = (ctx_index * row_count + jnp.arange(row_count, dtype=jnp.int32)) // BLOCK
    expert_ids = jnp.arange(EXPERTS, dtype=jnp.int32)
    stat_shape = (KVH, group_size, row_count)
    sums = [
        jnp.zeros((model_width,), jnp.float32),
        jnp.zeros((model_width,), jnp.float32),
        jnp.zeros((model_width, H * HD), jnp.float32),
        jnp.zeros((model_width, KVH * HD), jnp.float32),
        jnp.zeros((model_width, KVH * HD), jnp.float32),
        jnp.zeros((H * HD, model_width), jnp.float32),
        jnp.zeros((model_width, EXPERTS), jnp.float32),
        jnp.zeros((local_experts, model_width, FF), jnp.float32),
        jnp.zeros((local_experts, model_width, FF), jnp.float32),
        jnp.zeros((local_experts, FF, model_width), jnp.float32),
    ]
    outputs = []
    input_grads = []
    for micro_step in range(micro_count):
        weights = fetch(
            norm_one, norm_two, w_query, w_key, w_value, w_out, w_router, w_gate, w_up, w_down
        )
        gain_one = weights[0].astype(jnp.float32)
        gain_two = weights[1].astype(jnp.float32)
        query_full, key_full, value_full, out_full, router_full = (
            weights[2],
            weights[3],
            weights[4],
            weights[5],
            weights[6],
        )
        gate_full, up_full, down_full = (weights[7], weights[8], weights[9])
        inputs_f = tokens[micro_step, 0].astype(jnp.float32)
        normed_one, factor_one = normalize(inputs_f)
        normed_in = (normed_one * gain_one).astype(jnp.bfloat16)
        query_pre = jnp.dot(normed_in, query_full, preferred_element_type=jnp.float32)
        key_pre = jnp.dot(normed_in, key_full, preferred_element_type=jnp.float32)
        value_pre = jnp.dot(normed_in, value_full, preferred_element_type=jnp.float32)
        query_rot = rotate(query_pre.reshape(row_count, H, HD), cosine, sine, True).astype(
            jnp.bfloat16
        )
        query_grid = query_rot.reshape(row_count, KVH, group_size, HD)
        key_rot = (
            rotate(key_pre.reshape(row_count, KVH, HD), cosine, sine, True)
            .astype(jnp.bfloat16)
            .reshape(row_count, KVH * HD)
        )
        value_low = value_pre.astype(jnp.bfloat16)
        key_all, value_all = (
            lax.all_gather(key_rot, "ctx", axis=0, tiled=True),
            lax.all_gather(value_low, "ctx", axis=0, tiled=True),
        )

        def gather_stats(shard_at, carry):
            row_top, row_total = carry
            scores, unused = piece_scores(query_grid, key_all, shard_at, row_count, query_ids)
            new_top = jnp.maximum(row_top, jnp.max(scores, -1))
            row_total = row_total * jnp.exp(row_top - new_top) + jnp.sum(
                jnp.exp(scores - new_top[..., None]), -1
            )
            return (new_top, row_total)

        row_top, row_total = lax.fori_loop(
            0,
            ctx_index + 1,
            gather_stats,
            (jnp.full(stat_shape, NEGATIVE, jnp.float32), jnp.zeros(stat_shape, jnp.float32)),
        )

        def gather_output(shard_at, mixed):
            scores, unused = piece_scores(query_grid, key_all, shard_at, row_count, query_ids)
            probs = (jnp.exp(scores - row_top[..., None]) / row_total[..., None]).astype(
                jnp.bfloat16
            )
            value_piece = value_slice(value_all, shard_at, row_count)
            return mixed + jnp.einsum(
                "kgqt,tkd->qkgd", probs, value_piece, preferred_element_type=jnp.float32
            )

        attended = lax.fori_loop(
            0,
            ctx_index + 1,
            gather_output,
            jnp.zeros((row_count, KVH, group_size, HD), jnp.float32),
        ).reshape(row_count, H * HD)
        attended_low = attended.astype(jnp.bfloat16)
        hidden_one = inputs_f + RESIDUAL_MULT * jnp.dot(
            attended_low, out_full, preferred_element_type=jnp.float32
        )
        normed_two, factor_two = normalize(hidden_one)
        moe_in = (normed_two * gain_two).astype(jnp.bfloat16)
        logits = jnp.dot(moe_in, router_full, preferred_element_type=jnp.float32)
        chosen = routes[micro_step, 0]
        picks = chosen[..., None] == expert_ids[None, None, :]
        selected = jnp.sum(jnp.where(picks, logits[:, None, :], 0.0), -1)
        gate_probs = jax.nn.softmax(selected, -1)
        one_hot = picks.reshape(row_count * TOPK, EXPERTS).astype(jnp.int32)
        before = jnp.cumsum(one_hot, 0, dtype=jnp.int32) - one_hot
        pair_rank = jnp.sum(before * one_hot, -1, dtype=jnp.int32)
        slot_index = jnp.where(pair_rank < CAP, chosen.reshape(-1) * CAP + pair_rank, expert_slots)
        pair_rows = jnp.repeat(moe_in, TOPK, axis=0)
        send_rows = (
            jnp.zeros((expert_slots + 1, model_width), jnp.bfloat16).at[slot_index].set(pair_rows)
        )
        send_rows = send_rows[:expert_slots].reshape(EXPERTS, CAP, model_width)
        received = lax.all_to_all(send_rows, "exp", split_axis=0, concat_axis=1, tiled=True)
        gate_h = jnp.einsum("erd,edf->erf", received, gate_full, preferred_element_type=jnp.float32)
        up_h = jnp.einsum("erd,edf->erf", received, up_full, preferred_element_type=jnp.float32)
        sigma = jax.nn.sigmoid(gate_h)
        silu_gate = gate_h * sigma
        hidden_low = (silu_gate * up_h).astype(jnp.bfloat16)
        expert_out = jnp.einsum(
            "erf,efd->erd", hidden_low, down_full, preferred_element_type=jnp.float32
        ).astype(jnp.bfloat16)
        returned = lax.all_to_all(expert_out, "exp", split_axis=1, concat_axis=0, tiled=True)
        table = jnp.concatenate(
            [
                returned.reshape(expert_slots, model_width),
                jnp.zeros((1, model_width), jnp.bfloat16),
            ],
            0,
        )
        pair_out = table[slot_index].reshape(row_count, TOPK, model_width).astype(jnp.float32)
        result = hidden_one + RESIDUAL_MULT * jnp.sum(gate_probs[..., None] * pair_out, 1)
        outputs.append(result.astype(jnp.bfloat16))
        weights_back = fetch(
            norm_one, norm_two, w_query, w_key, w_value, w_out, w_router, w_gate, w_up, w_down
        )
        query_full, key_full, value_full, out_full, router_full = (
            weights_back[2],
            weights_back[3],
            weights_back[4],
            weights_back[5],
            weights_back[6],
        )
        gate_full, up_full, down_full = (weights_back[7], weights_back[8], weights_back[9])
        grad_out = cotangent[micro_step, 0].astype(jnp.float32)
        scaled_out = RESIDUAL_MULT * grad_out
        gate_sens = jnp.sum(pair_out * scaled_out[:, None, :], -1)
        pair_grad = (
            (gate_probs[..., None] * scaled_out[:, None, :])
            .astype(jnp.bfloat16)
            .reshape(row_count * TOPK, model_width)
        )
        send_grad = (
            jnp.zeros((expert_slots + 1, model_width), jnp.bfloat16).at[slot_index].set(pair_grad)
        )
        send_grad = send_grad[:expert_slots].reshape(EXPERTS, CAP, model_width)
        grad_recv = lax.all_to_all(send_grad, "exp", split_axis=0, concat_axis=1, tiled=True)
        inner = jnp.einsum("erd,efd->erf", grad_recv, down_full, preferred_element_type=jnp.float32)
        gate_d = (inner * up_h * sigma * (1.0 + gate_h * (1.0 - sigma))).astype(jnp.bfloat16)
        up_d = (inner * silu_gate).astype(jnp.bfloat16)
        sums[9] = sums[9] + jnp.einsum(
            "erf,erd->efd", hidden_low, grad_recv, preferred_element_type=jnp.float32
        )
        sums[7] = sums[7] + jnp.einsum(
            "erd,erf->edf", received, gate_d, preferred_element_type=jnp.float32
        )
        sums[8] = sums[8] + jnp.einsum(
            "erd,erf->edf", received, up_d, preferred_element_type=jnp.float32
        )
        expert_in_grad = (
            jnp.einsum("erf,edf->erd", gate_d, gate_full, preferred_element_type=jnp.float32)
            + jnp.einsum("erf,edf->erd", up_d, up_full, preferred_element_type=jnp.float32)
        ).astype(jnp.bfloat16)
        back_rows = lax.all_to_all(expert_in_grad, "exp", split_axis=1, concat_axis=0, tiled=True)
        back_table = jnp.concatenate(
            [
                back_rows.reshape(expert_slots, model_width),
                jnp.zeros((1, model_width), jnp.bfloat16),
            ],
            0,
        )
        moe_in_grad = jnp.sum(
            back_table[slot_index].reshape(row_count, TOPK, model_width).astype(jnp.float32), 1
        )
        gate_sel = gate_probs * (gate_sens - jnp.sum(gate_probs * gate_sens, -1, keepdims=True))
        logit_grad = jnp.sum(jnp.where(picks, gate_sel[..., None], 0.0), 1).astype(jnp.bfloat16)
        sums[6] = sums[6] + jnp.dot(moe_in.T, logit_grad, preferred_element_type=jnp.float32)
        moe_in_grad = moe_in_grad + jnp.dot(
            logit_grad, router_full.T, preferred_element_type=jnp.float32
        )
        sums[1] = sums[1] + jnp.sum(moe_in_grad * normed_two, 0)
        scaled_two = moe_in_grad * gain_two
        hidden_grad = grad_out + factor_two * (
            scaled_two - normed_two * jnp.mean(scaled_two * normed_two, -1, keepdims=True)
        )
        branch_grad = (RESIDUAL_MULT * hidden_grad).astype(jnp.bfloat16)
        sums[5] = sums[5] + jnp.dot(attended_low.T, branch_grad, preferred_element_type=jnp.float32)
        attended_grad = jnp.dot(branch_grad, out_full.T, preferred_element_type=jnp.float32).astype(
            jnp.bfloat16
        )
        attn_grad_grid = attended_grad.reshape(row_count, KVH, group_size, HD)
        delta = jnp.sum(
            (attended_grad.astype(jnp.float32) * attended).reshape(row_count, KVH, group_size, HD),
            -1,
        )
        delta = jnp.transpose(delta, (1, 2, 0))

        def gather_grads(shard_at, carry):
            query_acc, key_buffer, value_buffer = carry
            scores, key_piece = piece_scores(query_grid, key_all, shard_at, row_count, query_ids)
            value_piece = value_slice(value_all, shard_at, row_count)
            probs = jnp.exp(scores - row_top[..., None]) / row_total[..., None]
            probs_low = probs.astype(jnp.bfloat16)
            prob_grad = jnp.einsum(
                "qkgd,tkd->kgqt", attn_grad_grid, value_piece, preferred_element_type=jnp.float32
            )
            score_grad = (probs * (prob_grad - delta[..., None])).astype(jnp.bfloat16)
            query_acc = (
                query_acc
                + jnp.einsum(
                    "kgqt,tkd->qkgd", score_grad, key_piece, preferred_element_type=jnp.float32
                )
                * score_scale
            )
            key_part = (
                jnp.einsum(
                    "kgqt,qkgd->tkd", score_grad, query_grid, preferred_element_type=jnp.float32
                )
                * score_scale
            )
            value_part = jnp.einsum(
                "kgqt,qkgd->tkd", probs_low, attn_grad_grid, preferred_element_type=jnp.float32
            )
            first_row = shard_at * row_count
            key_buffer = lax.dynamic_update_slice_in_dim(
                key_buffer, key_part.reshape(row_count, KVH * HD), first_row, 0
            )
            value_buffer = lax.dynamic_update_slice_in_dim(
                value_buffer, value_part.reshape(row_count, KVH * HD), first_row, 0
            )
            return (query_acc, key_buffer, value_buffer)

        query_acc, key_buffer, value_buffer = lax.fori_loop(
            0,
            ctx_index + 1,
            gather_grads,
            (
                jnp.zeros((row_count, KVH, group_size, HD), jnp.float32),
                jnp.zeros((ctx_count * row_count, KVH * HD), jnp.float32),
                jnp.zeros((ctx_count * row_count, KVH * HD), jnp.float32),
            ),
        )
        key_sens, value_sens = (
            lax.psum_scatter(
                key_buffer.astype(jnp.bfloat16), "ctx", scatter_dimension=0, tiled=True
            ).astype(jnp.float32),
            lax.psum_scatter(
                value_buffer.astype(jnp.bfloat16), "ctx", scatter_dimension=0, tiled=True
            ).astype(jnp.float32),
        )
        query_low_grad = (
            rotate(query_acc.reshape(row_count, H, HD), cosine, sine, False)
            .reshape(row_count, H * HD)
            .astype(jnp.bfloat16)
        )
        key_low_grad = (
            rotate(key_sens.reshape(row_count, KVH, HD), cosine, sine, False)
            .reshape(row_count, KVH * HD)
            .astype(jnp.bfloat16)
        )
        value_low_grad = value_sens.astype(jnp.bfloat16)
        sums[2] = sums[2] + jnp.dot(normed_in.T, query_low_grad, preferred_element_type=jnp.float32)
        sums[3] = sums[3] + jnp.dot(normed_in.T, key_low_grad, preferred_element_type=jnp.float32)
        sums[4] = sums[4] + jnp.dot(normed_in.T, value_low_grad, preferred_element_type=jnp.float32)
        in_sens = (
            jnp.dot(query_low_grad, query_full.T, preferred_element_type=jnp.float32)
            + jnp.dot(key_low_grad, key_full.T, preferred_element_type=jnp.float32)
            + jnp.dot(value_low_grad, value_full.T, preferred_element_type=jnp.float32)
        )
        sums[0] = sums[0] + jnp.sum(in_sens * normed_one, 0)
        scaled_one = in_sens * gain_one
        token_grad = hidden_grad + factor_one * (
            scaled_one - normed_one * jnp.mean(scaled_one * normed_one, -1, keepdims=True)
        )
        input_grads.append(token_grad.astype(jnp.bfloat16))
    attention_shards = (
        lax.psum_scatter(
            sums[0].astype(jnp.bfloat16), ("dp", "ctx"), scatter_dimension=0, tiled=True
        ).astype(jnp.float32),
        lax.psum_scatter(
            sums[1].astype(jnp.bfloat16), ("dp", "ctx"), scatter_dimension=0, tiled=True
        ).astype(jnp.float32),
        lax.psum_scatter(
            sums[2].astype(jnp.bfloat16), ("dp", "ctx"), scatter_dimension=0, tiled=True
        ).astype(jnp.float32),
        lax.psum_scatter(
            sums[3].astype(jnp.bfloat16), ("dp", "ctx"), scatter_dimension=0, tiled=True
        ).astype(jnp.float32),
        lax.psum_scatter(
            sums[4].astype(jnp.bfloat16), ("dp", "ctx"), scatter_dimension=0, tiled=True
        ).astype(jnp.float32),
        lax.psum_scatter(
            sums[5].astype(jnp.bfloat16), ("dp", "ctx"), scatter_dimension=0, tiled=True
        ).astype(jnp.float32),
        lax.psum_scatter(
            sums[6].astype(jnp.bfloat16), ("dp", "ctx"), scatter_dimension=0, tiled=True
        ).astype(jnp.float32),
    )
    attention_shards = (
        lax.psum(attention_shards[0].astype(jnp.bfloat16), "exp").astype(jnp.float32),
        lax.psum(attention_shards[1].astype(jnp.bfloat16), "exp").astype(jnp.float32),
        lax.psum(attention_shards[2].astype(jnp.bfloat16), "exp").astype(jnp.float32),
        lax.psum(attention_shards[3].astype(jnp.bfloat16), "exp").astype(jnp.float32),
        lax.psum(attention_shards[4].astype(jnp.bfloat16), "exp").astype(jnp.float32),
        lax.psum(attention_shards[5].astype(jnp.bfloat16), "exp").astype(jnp.float32),
        lax.psum(attention_shards[6].astype(jnp.bfloat16), "exp").astype(jnp.float32),
    )
    expert_shards = (
        lax.psum_scatter(
            sums[7].astype(jnp.bfloat16), ("dp", "ctx"), scatter_dimension=1, tiled=True
        ).astype(jnp.float32),
        lax.psum_scatter(
            sums[8].astype(jnp.bfloat16), ("dp", "ctx"), scatter_dimension=1, tiled=True
        ).astype(jnp.float32),
        lax.psum_scatter(
            sums[9].astype(jnp.bfloat16), ("dp", "ctx"), scatter_dimension=2, tiled=True
        ).astype(jnp.float32),
    )
    layer_out = jnp.stack(outputs)[:, None]
    input_grad = jnp.stack(input_grads)[:, None]
    return (
        layer_out,
        input_grad,
        attention_shards[0],
        attention_shards[1],
        attention_shards[2],
        attention_shards[3],
        attention_shards[4],
        attention_shards[5],
        attention_shards[6],
        expert_shards[0],
        expert_shards[1],
        expert_shards[2],
    )


def solution(mesh):
    return jax.shard_map(
        on_device,
        mesh=mesh,
        in_specs=(
            P(None, ("dp", "exp"), "ctx", None),
            P(None, ("dp", "exp"), "ctx", None),
            P(None, ("dp", "exp"), "ctx", None),
            P(("dp", "ctx")),
            P(("dp", "ctx")),
            P(("dp", "ctx"), None),
            P(("dp", "ctx"), None),
            P(("dp", "ctx"), None),
            P(("dp", "ctx"), None),
            P(("dp", "ctx"), None),
            P("exp", ("dp", "ctx"), None),
            P("exp", ("dp", "ctx"), None),
            P("exp", None, ("dp", "ctx")),
        ),
        out_specs=(
            P(None, ("dp", "exp"), "ctx", None),
            P(None, ("dp", "exp"), "ctx", None),
            P(("dp", "ctx")),
            P(("dp", "ctx")),
            P(("dp", "ctx"), None),
            P(("dp", "ctx"), None),
            P(("dp", "ctx"), None),
            P(("dp", "ctx"), None),
            P(("dp", "ctx"), None),
            P("exp", ("dp", "ctx"), None),
            P("exp", ("dp", "ctx"), None),
            P("exp", None, ("dp", "ctx")),
        ),
        check_vma=False,
    )
```

profile of v0, /device:TPU:0, one launch (start us, length us, event | category | flops | bytes accessed | tf_op | source)
XLA Modules:
  0.0 1960.8 jit_solution(15295598635555771193)
XLA Ops:
  20.6 15.6 all-gather.14.cloned.1.call-done
  42.9 18.6 all-gather.18.cloned.1.call-done
  101.5 27.4 %all-gather.22.cloned.1.call-done = bf16[1024,1024]{1,0:T(8,128)(2,1)} async-done(((bf16[128,1024]{1,0:T(8,128)(2,1)}), bf16[1024,1024]{1,0:T(8,128)(2,1)}) %all-gather.22.cloned.1.call-update) | async-done | bytes 2097168 | tf_op jit(solution)/shard_map/all_gather | solution.py:72
  154.8 22.7 %all-gather.24.cloned.1.call-done = bf16[1024,1024]{1,0:T(8,128)(2,1)} async-done(((bf16[128,1024]{1,0:T(8,128)(2,1)}), bf16[1024,1024]{1,0:T(8,128)(2,1)}) %all-gather.24.cloned.1.call-update) | async-done | bytes 2097168 | tf_op jit(solution)/shard_map/all_gather | solution.py:75
  180.3 16.2 all-gather.34.cloned.1.call-done
  209.9 12.7 scatter_custom_fusion
  234.3 30.0 %all_gather.36 = bf16[1024,32]{0,1:T(8,128)(2,1)S(1)} all-gather(bf16[128,32]{0,1:T(8,128)(2,1)S(1)} %copy-done.76), channel_id=1, replica_groups=mesh['dp'=2,'ctx'=4,'exp'=4] {'dp','ctx'}, dimensions={0}, use_global_device_ids=true | all-gather | bytes 73728 | tf_op jit(solution)/shard_map/all_gather | solution.py:76
  267.3 13.9 scatter_custom_fusion.2
  287.2 51.1 %all-to-all-done = bf16[32,72,1024]{2,1,0:T(8,128)(2,1)} async-done(((bf16[32,72,1024]{2,1,0:T(8,128)(2,1)}), bf16[32,72,1024]{2,1,0:T(8,128)(2,1)}, u32[]{:S(2)}, u32[]{:S(2)}) %all-to-all-start) | async-done | bytes 4718624 | tf_op jit(solution)/shard_map/all_to_all | solution.py:215
  348.5 100.6 %all-to-all-done.4 = bf16[32,72,1024]{2,1,0:T(8,128)(2,1)} async-done(((bf16[32,72,1024]{2,1,0:T(8,128)(2,1)}), bf16[32,72,1024]{2,1,0:T(8,128)(2,1)}, u32[]{:S(2)}, u32[]{:S(2)}) %all-to-all-start.4) | async-done | bytes 4718624 | tf_op jit(solution)/shard_map/all_to_all | solution.py:258
  473.4 11.1 multiply_convert_fusion.2
  484.5 13.2 fusion.177
  497.7 11.6 add_convert_fusion.4
  532.4 93.9 %all-to-all-done.5 = bf16[8,288,1024]{2,0,1:T(8,128)(2,1)} async-done(((bf16[8,288,1024]{2,0,1:T(8,128)(2,1)}), bf16[8,288,1024]{2,0,1:T(8,128)(2,1)}, u32[]{:S(2)}, u32[]{:S(2)}) %all-to-all-start.5) | async-done | bytes 4718624 | tf_op jit(solution)/shard_map/all_to_all | solution.py:275
  649.4 14.3 gather_fusion.2
  670.3 65.0 %all-to-all-done.1 = bf16[8,288,1024]{2,0,1:T(8,128)(2,1)} async-done(((bf16[8,288,1024]{2,0,1:T(8,128)(2,1)}), bf16[8,288,1024]{2,0,1:T(8,128)(2,1)}, u32[]{:S(2)}, u32[]{:S(2)}) %all-to-all-start.1) | async-done | bytes 4718624 | tf_op jit(solution)/shard_map/all_to_all | solution.py:224
  742.9 14.1 gather_fusion
  766.6 12.9 scatter_custom_fusion.1
  790.2 13.5 scatter_custom_fusion.3
  808.7 84.8 %all-to-all-done.2 = bf16[32,72,1024]{2,1,0:T(8,128)(2,1)} async-done(((bf16[32,72,1024]{2,1,0:T(8,128)(2,1)}), bf16[32,72,1024]{2,1,0:T(8,128)(2,1)}, u32[]{:S(2)}, u32[]{:S(2)}) %all-to-all-start.2) | async-done | bytes 4718624 | tf_op jit(solution)/shard_map/all_to_all | solution.py:215
  903.9 98.7 %all-to-all-done.6 = bf16[32,72,1024]{2,1,0:T(8,128)(2,1)} async-done(((bf16[32,72,1024]{2,1,0:T(8,128)(2,1)}), bf16[32,72,1024]{2,1,0:T(8,128)(2,1)}, u32[]{:S(2)}, u32[]{:S(2)}) %all-to-all-start.6) | async-done | bytes 4718624 | tf_op jit(solution)/shard_map/all_to_all | solution.py:258
  1020.4 11.9 multiply_convert_fusion
  1039.0 11.6 add_convert_fusion.3
  1074.3 92.9 %all-to-all-done.7 = bf16[8,288,1024]{2,0,1:T(8,128)(2,1)} async-done(((bf16[8,288,1024]{2,0,1:T(8,128)(2,1)}), bf16[8,288,1024]{2,0,1:T(8,128)(2,1)}, u32[]{:S(2)}, u32[]{:S(2)}) %all-to-all-start.7) | async-done | bytes 4718624 | tf_op jit(solution)/shard_map/all_to_all | solution.py:275
  1182.5 14.1 gather_fusion.3
  1203.0 73.1 %all-to-all-done.3 = bf16[8,288,1024]{2,0,1:T(8,128)(2,1)} async-done(((bf16[8,288,1024]{2,0,1:T(8,128)(2,1)}), bf16[8,288,1024]{2,0,1:T(8,128)(2,1)}, u32[]{:S(2)}, u32[]{:S(2)}) %all-to-all-start.3) | async-done | bytes 4718624 | tf_op jit(solution)/shard_map/all_to_all | solution.py:224
  1283.7 14.1 gather_fusion.1
  1348.4 38.3 %reduce-scatter.17.cloned.1.call-done = bf16[256,512]{0,1:T(8,128)(2,1)} async-done(((bf16[1024,512]{0,1:T(8,128)(2,1)}), bf16[256,512]{0,1:T(8,128)(2,1)}) %reduce-scatter.17.cloned.1.call-update) | async-done | bytes 262160 | tf_op jit(solution)/shard_map/reduce_scatter | solution.py:355
  1387.7 29.8 %reduce-scatter.21.cloned.1.call-done = bf16[256,512]{0,1:T(8,128)(2,1)} async-done(((bf16[1024,512]{0,1:T(8,128)(2,1)}), bf16[256,512]{0,1:T(8,128)(2,1)}) %reduce-scatter.21.cloned.1.call-update) | async-done | bytes 262160 | tf_op jit(solution)/shard_map/reduce_scatter | solution.py:355
  1421.8 23.1 %reduce-scatter.19.cloned.1.call-done = bf16[256,512]{0,1:T(8,128)(2,1)} async-done(((bf16[1024,512]{0,1:T(8,128)(2,1)}), bf16[256,512]{0,1:T(8,128)(2,1)}) %reduce-scatter.19.cloned.1.call-update) | async-done | bytes 262160 | tf_op jit(solution)/shard_map/reduce_scatter | solution.py:358
  1447.7 24.6 %reduce-scatter.23.cloned.1.call-done = bf16[256,512]{0,1:T(8,128)(2,1)} async-done(((bf16[1024,512]{0,1:T(8,128)(2,1)}), bf16[256,512]{0,1:T(8,128)(2,1)}) %reduce-scatter.23.cloned.1.call-update) | async-done | bytes 262160 | tf_op jit(solution)/shard_map/reduce_scatter | solution.py:358
  1479.1 10.8 fusion.183
  1489.9 27.4 %reduce-scatter.25.cloned.1.call-done = bf16[128,1024]{1,0:T(8,128)(2,1)} async-done(((bf16[1024,1024]{1,0:T(8,128)(2,1)}), bf16[128,1024]{1,0:T(8,128)(2,1)}) %reduce-scatter.25.cloned.1.call-update) | async-done | bytes 262160 | tf_op jit(solution)/shard_map/reduce_scatter | solution.py:394
  1517.3 45.3 %reduce-scatter.31.cloned.1.call-done = bf16[128,1024]{1,0:T(8,128)(2,1)} async-done(((bf16[1024,1024]{1,0:T(8,128)(2,1)}), bf16[128,1024]{1,0:T(8,128)(2,1)}) %reduce-scatter.31.cloned.1.call-update) | async-done | bytes 262160 | tf_op jit(solution)/shard_map/reduce_scatter | solution.py:403
  1562.7 39.6 %reduce-scatter.27.cloned.1.call-done = bf16[128,512]{1,0:T(8,128)(2,1)} async-done(((bf16[1024,512]{1,0:T(8,128)(2,1)}), bf16[128,512]{1,0:T(8,128)(2,1)}) %reduce-scatter.27.cloned.1.call-update) | async-done | bytes 131088 | tf_op jit(solution)/shard_map/reduce_scatter | solution.py:397
  1602.3 39.8 %reduce-scatter.29.cloned.1.call-done = bf16[128,512]{1,0:T(8,128)(2,1)} async-done(((bf16[1024,512]{1,0:T(8,128)(2,1)}), bf16[128,512]{1,0:T(8,128)(2,1)}) %reduce-scatter.29.cloned.1.call-update) | async-done | bytes 131088 | tf_op jit(solution)/shard_map/reduce_scatter | solution.py:400
  1642.3 15.7 add_convert_fusion
  1658.0 12.7 copy.273
  1670.7 12.2 copy.277
  1684.6 11.2 fusion.181
  1695.9 12.3 add_convert_fusion.2
  1709.9 11.3 fusion.182
  1721.2 12.3 add_convert_fusion.1
  1751.9 13.1 all-reduce.6
  1765.2 11.9 all-reduce.7
  1788.8 12.3 reduce-scatter.39.cloned.1.call-done
  1805.2 70.7 %reduce-scatter.33.cloned.1.call-done = bf16[8,128,512]{2,1,0:T(8,128)(2,1)} async-done(((bf16[8,1024,512]{2,1,0:T(8,128)(2,1)}), bf16[8,128,512]{2,1,0:T(8,128)(2,1)}) %reduce-scatter.33.cloned.1.call-update) | async-done | bytes 1048592 | tf_op jit(solution)/shard_map/reduce_scatter | solution.py:420
  1878.7 72.2 %reduce-scatter.35.cloned.1.call-done = bf16[8,128,512]{2,1,0:T(8,128)(2,1)} async-done(((bf16[8,1024,512]{2,1,0:T(8,128)(2,1)}), bf16[8,128,512]{2,1,0:T(8,128)(2,1)}) %reduce-scatter.35.cloned.1.call-update) | async-done | bytes 1048592 | tf_op jit(solution)/shard_map/reduce_scatter | solution.py:423
  (472 shorter events, 465.4 us)
Async XLA Ops:
  7.2 28.9 %all-gather.14.cloned.1.call-start = ((), (), s32[]{:S(2)}) async-start(), calls=%async_computation.20 | async-start | bytes 1179648 | tf_op jit(solution)/shard_map/all_gather | solution.py:74
  7.9 53.6 %all-gather.18.cloned.1.call-start = ((), (), s32[]{:S(2)}) async-start(), calls=%async_computation.22 | async-start | bytes 1179648 | tf_op jit(solution)/shard_map/all_gather | solution.py:73
  8.7 79.4 %all-gather.16.cloned.1.call-start = ((), (), s32[]{:S(2)}) async-start(), calls=%async_computation.21 | async-start | bytes 1310720 | tf_op jit(solution)/shard_map/all_gather | solution.py:160
  19.0 116.4 %copy-start.61 = (f32[8,1,128]{2,1,0:T(1,128)}, f32[8,1,128]{2,1,0:T(1,128)S(1)}, u32[]{:S(2)}) copy-start(f32[8,1,128]{2,1,0:T(1,128)S(1)} %convert_element_type.516) | copy-start | bytes 12292
  20.5 42.5 %copy-start.5 = (bf16[2,1,256,1024]{3,2,1,0:T(8,128)(2,1)S(1)}, bf16[2,1,256,1024]{3,2,1,0:T(8,128)(2,1)}, u32[]{:S(2)}) copy-start(bf16[2,1,256,1024]{3,2,1,0:T(8,128)(2,1)} %param.25) | copy-start | bytes 3145732
  20.6 112.3 %copy-start.69 = (f32[256]{0:T(256)}, f32[256]{0:T(256)S(1)}, u32[]{:S(2)}) copy-start(f32[256]{0:T(256)S(1)} %add_rsqrt_fusion.3) | copy-start | bytes 3076
  38.7 60.5 %all-gather.32.cloned.1.call-start = ((), (), s32[]{:S(2)}) async-start(), calls=%async_computation.29 | async-start | bytes 1310720 | tf_op jit(solution)/shard_map/all_gather | solution.py:160
  38.8 96.6 %copy-start.71 = (f32[256]{0:T(256)}, f32[256]{0:T(256)S(1)}, u32[]{:S(2)}) copy-start(f32[256]{0:T(256)S(1)} %add_rsqrt_fusion.1) | copy-start | bytes 3076
  41.4 87.5 %all-gather.22.cloned.1.call-start = ((), (), s32[]{:S(2)}) async-start(), calls=%async_computation.24 | async-start | bytes 2359296 | tf_op jit(solution)/shard_map/all_gather | solution.py:72
  42.0 105.7 %all-gather.20.cloned.1.call-start = ((), (), s32[]{:S(2)}) async-start(), calls=%async_computation.23 | async-start | bytes 1310720 | tf_op jit(solution)/shard_map/all_gather | solution.py:159
  42.9 93.4 %copy-start.54 = (f32[256,32]{0,1:T(8,128)}, f32[256,32]{0,1:T(8,128)S(1)}, u32[]{:S(2)}) copy-start(f32[256,32]{0,1:T(8,128)S(1)} %get-tuple-element.1408) | copy-start | bytes 98308
  65.1 112.5 %all-gather.24.cloned.1.call-start = ((), (), s32[]{:S(2)}) async-start(), calls=%async_computation.25 | async-start | bytes 2359296 | tf_op jit(solution)/shard_map/all_gather | solution.py:75
  65.8 130.7 %all-gather.34.cloned.1.call-start = ((), (), s32[]{:S(2)}) async-start(), calls=%async_computation.30 | async-start | bytes 1310720 | tf_op jit(solution)/shard_map/all_gather | solution.py:159
  66.6 387.7 %all-gather.26.cloned.1.call-start = ((), (), s32[]{:S(2)}) async-start(), calls=%async_computation.26 | async-start | bytes 9437184 | tf_op jit(solution)/shard_map/all_gather | solution.py:79
  67.4 396.5 %all-gather.28.cloned.1.call-start = ((), (), s32[]{:S(2)}) async-start(), calls=%async_computation.27 | async-start | bytes 9437184 | tf_op jit(solution)/shard_map/all_gather | solution.py:80
  153.6 43.0 %copy-start.1 = (bf16[256,8,2,64]{0,3,2,1:T(8,128)(2,1)}, bf16[256,8,2,64]{0,3,2,1:T(8,128)(2,1)S(1)}, u32[]{:S(2)}) copy-start(bf16[256,8,2,64]{0,3,2,1:T(8,128)(2,1)S(1)} %get-tuple-element.2103) | copy-start | bytes 1572868
  153.6 43.0 %copy-start.56 = (f32[8,2,256]{2,1,0:T(2,128)}, f32[8,2,256]{2,1,0:T(2,128)S(1)}, u32[]{:S(2)}) copy-start(f32[8,2,256]{2,1,0:T(2,128)S(1)} %get-tuple-element.2176) | copy-start | bytes 49156
  209.9 56.8 %copy-start.34 = (bf16[256,1024]{1,0:T(8,128)(2,1)}, bf16[256,1024]{1,0:T(8,128)(2,1)S(1)}, u32[]{:S(2)}) copy-start(bf16[256,1024]{1,0:T(8,128)(2,1)S(1)} %multiply_convert_fusion.9) | copy-start | bytes 1572868
  228.4 109.9 %all-to-all-start = ((bf16[32,72,1024]{2,1,0:T(8,128)(2,1)}), bf16[32,72,1024]{2,1,0:T(8,128)(2,1)}, u32[]{:S(2)}, u32[]{:S(2)}) async-start(bf16[32,72,1024]{2,1,0:T(8,128)(2,1)} %bitcast.736), calls=%async_computation | async-start | bytes 9437184 | tf_op jit(solution)/shard_map/all_to_all | solution.py:215
  233.5 239.9 %all-gather.30.cloned.1.call-start = ((), (), s32[]{:S(2)}) async-start(), calls=%async_computation.28 | async-start | bytes 9437184 | tf_op jit(solution)/shard_map/all_gather | solution.py:81
  338.3 110.8 %all-to-all-start.4 = ((bf16[32,72,1024]{2,1,0:T(8,128)(2,1)}), bf16[32,72,1024]{2,1,0:T(8,128)(2,1)}, u32[]{:S(2)}, u32[]{:S(2)}) async-start(bf16[32,72,1024]{2,1,0:T(8,128)(2,1)} %bitcast.738), calls=%async_computation.4 | async-start | bytes 9437184 | tf_op jit(solution)/shard_map/all_to_all | solution.py:258
  484.5 36.8 %copy-start.8 = (bf16[8,288,512]{2,1,0:T(8,128)(2,1)}, bf16[8,288,512]{2,1,0:T(8,128)(2,1)S(1)}, u32[]{:S(2)}) copy-start(bf16[8,288,512]{2,1,0:T(8,128)(2,1)S(1)} %get-tuple-element.1363) | copy-start | bytes 7077892
  516.4 109.9 %all-to-all-start.5 = ((bf16[8,288,1024]{2,0,1:T(8,128)(2,1)}), bf16[8,288,1024]{2,0,1:T(8,128)(2,1)}, u32[]{:S(2)}, u32[]{:S(2)}) async-start(bf16[8,288,1024]{2,0,1:T(8,128)(2,1)} %copy.227), calls=%async_computation.5 | async-start | bytes 9437184 | tf_op jit(solution)/shard_map/all_to_all | solution.py:275
  532.4 98.9 %copy-start.68 = (s32[1,1,256,8]{2,3,1,0:T(8,128)S(1)}, s32[1,1,256,8]{2,3,1,0:T(8,128)}, u32[]{:S(2)}) copy-start(s32[1,1,256,8]{2,3,1,0:T(8,128)} %get-tuple-element.1403) | copy-start | bytes 24580
  532.4 108.9 %copy-start.67 = (s32[1,1,256,8]{2,3,1,0:T(8,128)S(1)}, s32[1,1,256,8]{2,3,1,0:T(8,128)}, u32[]{:S(2)}) copy-start(s32[1,1,256,8]{2,3,1,0:T(8,128)} %get-tuple-element.1402) | copy-start | bytes 24580
  626.2 109.0 %all-to-all-start.1 = ((bf16[8,288,1024]{2,0,1:T(8,128)(2,1)}), bf16[8,288,1024]{2,0,1:T(8,128)(2,1)}, u32[]{:S(2)}, u32[]{:S(2)}) async-start(bf16[8,288,1024]{2,0,1:T(8,128)(2,1)} %copy.213), calls=%async_computation.1 | async-start | bytes 9437184 | tf_op jit(solution)/shard_map/all_to_all | solution.py:224
  784.5 109.0 %all-to-all-start.2 = ((bf16[32,72,1024]{2,1,0:T(8,128)(2,1)}), bf16[32,72,1024]{2,1,0:T(8,128)(2,1)}, u32[]{:S(2)}, u32[]{:S(2)}) async-start(bf16[32,72,1024]{2,1,0:T(8,128)(2,1)} %bitcast.737), calls=%async_computation.2 | async-start | bytes 9437184 | tf_op jit(solution)/shard_map/all_to_all | solution.py:215
  893.5 109.1 %all-to-all-start.6 = ((bf16[32,72,1024]{2,1,0:T(8,128)(2,1)}), bf16[32,72,1024]{2,1,0:T(8,128)(2,1)}, u32[]{:S(2)}, u32[]{:S(2)}) async-start(bf16[32,72,1024]{2,1,0:T(8,128)(2,1)} %bitcast.739), calls=%async_computation.8 | async-start | bytes 9437184 | tf_op jit(solution)/shard_map/all_to_all | solution.py:258
  1057.7 109.4 %all-to-all-start.7 = ((bf16[8,288,1024]{2,0,1:T(8,128)(2,1)}), bf16[8,288,1024]{2,0,1:T(8,128)(2,1)}, u32[]{:S(2)}, u32[]{:S(2)}) async-start(bf16[8,288,1024]{2,0,1:T(8,128)(2,1)} %copy.237), calls=%async_computation.9 | async-start | bytes 9437184 | tf_op jit(solution)/shard_map/all_to_all | solution.py:275
  1074.3 97.9 %copy-start.14 = (f32[256,8,2,64]{0,3,2,1:T(8,128)S(1)}, f32[256,8,2,64]{0,3,2,1:T(8,128)}, u32[]{:S(2)}) copy-start(f32[256,8,2,64]{0,3,2,1:T(8,128)} %copy-done.13) | copy-start | bytes 3145732
  1074.3 99.3 %copy-start.19 = (f32[256,8,2,64]{0,3,2,1:T(8,128)S(1)}, f32[256,8,2,64]{0,3,2,1:T(8,128)}, u32[]{:S(2)}) copy-start(f32[256,8,2,64]{0,3,2,1:T(8,128)} %get-tuple-element.773) | copy-start | bytes 3145732
  1167.2 108.9 %all-to-all-start.3 = ((bf16[8,288,1024]{2,0,1:T(8,128)(2,1)}), bf16[8,288,1024]{2,0,1:T(8,128)(2,1)}, u32[]{:S(2)}, u32[]{:S(2)}) async-start(bf16[8,288,1024]{2,0,1:T(8,128)(2,1)} %copy.223), calls=%async_computation.3 | async-start | bytes 9437184 | tf_op jit(solution)/shard_map/all_to_all | solution.py:224
  1172.1 214.6 %reduce-scatter.17.cloned.1.call-start = ((), (), s32[]{:S(2)}) async-start(), calls=%async_computation.31 | async-start | bytes 1310720 | tf_op jit(solution)/shard_map/reduce_scatter | solution.py:355
  1329.8 87.7 %reduce-scatter.21.cloned.1.call-start = ((), (), s32[]{:S(2)}) async-start(), calls=%async_computation.33 | async-start | bytes 1310720 | tf_op jit(solution)/shard_map/reduce_scatter | solution.py:355
  1339.4 105.4 %reduce-scatter.19.cloned.1.call-start = ((), (), s32[]{:S(2)}) async-start(), calls=%async_computation.32 | async-start | bytes 1310720 | tf_op jit(solution)/shard_map/reduce_scatter | solution.py:358
  1340.0 132.3 %reduce-scatter.23.cloned.1.call-start = ((), (), s32[]{:S(2)}) async-start(), calls=%async_computation.34 | async-start | bytes 1310720 | tf_op jit(solution)/shard_map/reduce_scatter | solution.py:358
  1340.6 176.7 %reduce-scatter.25.cloned.1.call-start = ((), (), s32[]{:S(2)}) async-start(), calls=%async_computation.35 | async-start | bytes 2359296 | tf_op jit(solution)/shard_map/reduce_scatter | solution.py:394
  1344.7 218.0 %reduce-scatter.31.cloned.1.call-start = ((), (), s32[]{:S(2)}) async-start(), calls=%async_computation.38 | async-start | bytes 2359296 | tf_op jit(solution)/shard_map/reduce_scatter | solution.py:403
  1348.4 253.9 %reduce-scatter.27.cloned.1.call-start = ((), (), s32[]{:S(2)}) async-start(), calls=%async_computation.36 | async-start | bytes 1179648 | tf_op jit(solution)/shard_map/reduce_scatter | solution.py:397
  1421.7 53.9 %copy-start.65 = (bf16[256,32]{0,1:T(8,128)(2,1)S(1)}, bf16[256,32]{0,1:T(8,128)(2,1)}, u32[]{:S(2)}) copy-start(bf16[256,32]{0,1:T(8,128)(2,1)} %copy-done.64) | copy-start | bytes 49156
  1421.7 220.3 %reduce-scatter.29.cloned.1.call-start = ((), (), s32[]{:S(2)}) async-start(), calls=%async_computation.37 | async-start | bytes 1179648 | tf_op jit(solution)/shard_map/reduce_scatter | solution.py:400
  1447.7 31.4 %copy-start.9 = (bf16[8,288,512]{2,1,0:T(8,128)(2,1)S(1)}, bf16[8,288,512]{2,1,0:T(8,128)(2,1)}, u32[]{:S(2)}) copy-start(bf16[8,288,512]{2,1,0:T(8,128)(2,1)} %copy-done.8) | copy-start | bytes 7077892
  1475.6 266.8 %reduce-scatter.37.cloned.1.call-start = ((), (), s32[]{:S(2)}) async-start(), calls=%async_computation.41 | async-start | bytes 294912
  1479.0 302.9 %all-reduce.11.cloned.1.call-start = ((), (), s32[]{:S(2)}) async-start(), calls=%async_computation.43 | async-start | bytes 1572864 | tf_op jit(solution)/shard_map/psum | solution.py:413
  1642.1 159.0 %reduce-scatter.39.cloned.1.call-start = ((), (), s32[]{:S(2)}) async-start(), calls=%async_computation.42 | async-start | bytes 9437184
  1683.0 192.9 %reduce-scatter.33.cloned.1.call-start = ((), (), s32[]{:S(2)}) async-start(), calls=%async_computation.39 | async-start | bytes 9437184 | tf_op jit(solution)/shard_map/reduce_scatter | solution.py:420
  1708.2 242.7 %reduce-scatter.35.cloned.1.call-start = ((), (), s32[]{:S(2)}) async-start(), calls=%async_computation.40 | async-start | bytes 9437184 | tf_op jit(solution)/shard_map/reduce_scatter | solution.py:423
  1747.8 31.0 %copy-start.18 = (f32[256,1024]{1,0:T(8,128)S(1)}, f32[256,1024]{1,0:T(8,128)}, u32[]{:S(2)}) copy-start(f32[256,1024]{1,0:T(8,128)} %copy-done.16) | copy-start | bytes 3145732
  (67 other events, 541.6 us)
Sparse Core Ops, SparseCore 0:
  9.9 26.1 all-gather.13
  38.0 23.4 all-gather.17
  63.7 16.7 all-gather.15
  82.4 16.7 all-gather.31
  101.0 27.8 all-gather.21
  130.9 16.8 all-gather.19
  149.6 27.8 all-gather.23
  179.7 16.8 all-gather.33
  198.5 54.3 all-gather.25
  254.7 54.3 all-gather.27
  311.0 55.9 all-gather.29
  1330.0 56.7 reduce-scatter.16
  1390.0 27.5 reduce-scatter.20
  1420.0 24.8 reduce-scatter.18
  1447.4 24.8 reduce-scatter.22
  1476.1 41.2 reduce-scatter.24
  1521.4 41.2 reduce-scatter.30
  1566.3 35.9 reduce-scatter.26
  1606.0 35.9 reduce-scatter.28
  1645.5 33.5 reduce-scatter.36
  1681.9 44.6 all-reduce.10
  1730.5 70.5 reduce-scatter.38
  1804.6 71.2 reduce-scatter.32
  1879.6 71.2 reduce-scatter.34
where the time goes:
time: 1970 us; the launch traced here: 1960 us
  waiting for transfers between devices  1210 us (61%)
  matrix products  256 us (13%)
  local copies, waits for them, and re-layouts  249 us (13%)
  other arithmetic  113 us (6%)
  blocking collectives  74.1 us (4%)
  starting transfers between devices  42.5 us (2%)
    all_to_all x2, waiting for transfers between devices, on_device(): lax.all_to_all(send_grad, 'exp', split_axis=0, concat_axis=1, tiled=True)  199 us
    all_to_all x2, waiting for transfers between devices, on_device(): lax.all_to_all(expert_in_grad, 'exp', split_axis=1, concat_axis=0, tiled=...  187 us
    all_to_all x2, waiting for transfers between devices, on_device(): lax.all_to_all(expert_out, 'exp', split_axis=1, concat_axis=0, tiled=True)  138 us
    all_to_all x2, waiting for transfers between devices, on_device(): lax.all_to_all(send_rows, 'exp', split_axis=0, concat_axis=1, tiled=True)  136 us
    reduce_scatter x1, waiting for transfers between devices, on_device(): lax.psum_scatter(sums[8].astype(jnp.bfloat16), ('dp', 'ctx'), scatter_dim...  72.2 us
    reduce_scatter x1, waiting for transfers between devices, on_device(): lax.psum_scatter(sums[7].astype(jnp.bfloat16), ('dp', 'ctx'), scatter_dim...  70.7 us
    reduce_scatter x2, waiting for transfers between devices, on_device(): lax.psum_scatter(key_buffer.astype(jnp.bfloat16), 'ctx', scatter_dimensio...  68.2 us
    reduce_scatter x2, waiting for transfers between devices, on_device(): lax.psum_scatter(value_buffer.astype(jnp.bfloat16), 'ctx', scatter_dimens...  47.7 us
  transfers between devices with their start and end apart: 32, of which 26 were waited for; matrix products, arithmetic and copies ran while one was open for 21% of the time, Pallas kernels for 0%

commit v1 on v0

v1 whole, which is shorter than its diff:
```python
import jax
import jax.numpy as jnp
from jax import lax
from jax.experimental import pallas as pl
from jax.experimental.pallas import tpu as pltpu
from jax.sharding import PartitionSpec as P

H = 16
KVH = 8
HD = 64
EXPERTS = 32
FF = 512
TOPK = 8
BLOCK = 256
CAP = 72
GROUP = H // KVH

EPSILON = 1e-06
BASE_THETA = 10000.0
NEGATIVE = -1e30
ATTENTION_MULT = 0.015625
RESIDUAL_MULT = 0.22

PLANE = ("dp", "ctx")
BF = jnp.bfloat16
F32 = jnp.float32


def dot(left, right):
    return jnp.dot(left, right, preferred_element_type=F32)


def dot_tn(left, right):
    return lax.dot_general(left, right, (((0,), (0,)), ((), ())), preferred_element_type=F32)


def dot_nt(left, right):
    return lax.dot_general(left, right, (((1,), (1,)), ((), ())), preferred_element_type=F32)


def add(left, right):
    return left.astype(F32) + right.astype(F32)


def relative(blocks, index):
    count = len(blocks)
    bit = 1
    while bit < count:
        on = (index & bit) != 0
        blocks = [jnp.where(on, blocks[j ^ bit], blocks[j]) for j in range(count)]
        bit *= 2
    return blocks


def reorder(array, count, index, axis):
    return jnp.concatenate(relative(jnp.split(array, count, axis), index), axis)


def plane_swap(array, mask):
    count = lax.axis_size("dp") * lax.axis_size("ctx")
    return lax.ppermute(array, PLANE, [(i, i ^ mask) for i in range(count)])


def sibling(array):
    return plane_swap(array, 1)


def halves(array):
    return jnp.split(array, 2, -2)


def gather_chips(own):
    chips = lax.axis_size("dp") * lax.axis_size("ctx") // 2
    if chips == 4:
        along_x, along_y = plane_swap(own, 2), plane_swap(own, 4)
        first, last = halves(along_x)[0], halves(along_y)[1]
        far = jnp.concatenate([plane_swap(first, 4), plane_swap(last, 2)], -2)
        return [own, along_x, along_y, far]
    blocks, mask = [own], 1
    while mask < chips:
        blocks = blocks + [plane_swap(b, 2 * mask) for b in blocks]
        mask *= 2
    return blocks


def gather_plane(own):
    blocks = []
    for block in gather_chips(own):
        blocks += [block, sibling(block)]
    return blocks


def reduce_chips(blocks):
    chips = len(blocks)
    if chips == 4:
        upper, lower = zip(*[halves(b) for b in blocks])
        from_x = plane_swap(jnp.concatenate([upper[1], upper[3]], -2), 2)
        from_y = plane_swap(jnp.concatenate([lower[2], lower[3]], -2), 4)
        x_own, x_rest = halves(from_x)
        y_own, y_rest = halves(from_y)
        upper_last = plane_swap(add(upper[2], x_rest).astype(BF), 4)
        lower_last = plane_swap(add(lower[1], y_rest).astype(BF), 2)
        top = add(upper[0], x_own) + upper_last.astype(F32)
        low = add(lower[0], y_own) + lower_last.astype(F32)
        return jnp.concatenate([top, low], -2)
    mask = chips // 2
    while mask:
        blocks = [
            add(blocks[j], plane_swap(blocks[j + mask], 2 * mask)).astype(BF) for j in range(mask)
        ]
        mask //= 2
    return blocks[0].astype(F32)


def reduce_plane(blocks):
    other = sibling(jnp.concatenate(blocks[1::2], -2))
    others = jnp.split(other, len(blocks) // 2, -2)
    return reduce_chips([add(a, b).astype(BF) for a, b in zip(blocks[0::2], others)])


def gather_ctx(own):
    count = lax.axis_size("ctx")
    if count == 4:
        near = lax.ppermute(own, "ctx", [(0, 1), (2, 3)])
        along = lax.ppermute(own, "ctx", [(0, 2), (1, 3)])
        far = lax.ppermute(along, "ctx", [(2, 3), (3, 2)])
        return [own, near, along, far]
    blocks, mask = [own], 1
    while mask < count:
        blocks = blocks + [
            lax.ppermute(b, "ctx", [(i, i ^ mask) for i in range(count)]) for b in blocks
        ]
        mask *= 2
    return blocks


def reduce_ctx(blocks):
    count = lax.axis_size("ctx")
    if count == 4:
        far = lax.ppermute(blocks[3], "ctx", [(2, 3), (3, 2)])
        along = lax.ppermute(add(blocks[2], far).astype(BF), "ctx", [(2, 0), (3, 1)])
        near = lax.ppermute(blocks[1], "ctx", [(1, 0), (3, 2)])
        return add(blocks[0], near) + along.astype(F32)
    mask = count // 2
    while mask:
        perm = [(i, i ^ mask) for i in range(count)]
        blocks = [
            add(blocks[j], lax.ppermute(blocks[j + mask], "ctx", perm)).astype(BF)
            for j in range(mask)
        ]
        mask //= 2
    return blocks[0].astype(F32)


def ring_step(array):
    count = lax.axis_size("exp")
    return lax.ppermute(array, "exp", [(i, (i + 1) % count) for i in range(count)])


def gather_ring(own):
    blocks = [own]
    for _ in range(lax.axis_size("exp") - 1):
        blocks.append(ring_step(blocks[-1]))
    return blocks


def reduce_ring(blocks):
    count = len(blocks)
    total = blocks[1 % count]
    for k in range(2, count + 1):
        total = add(ring_step(total), blocks[k % count]).astype(BF)
    return total


def rotation(offset, row_count):
    half_size = HD // 2
    inverse = jnp.exp(jnp.arange(half_size, dtype=F32) * (-2.0 * jnp.log(F32(BASE_THETA)) / HD))
    places = (offset + jnp.arange(row_count, dtype=jnp.int32)).astype(F32)
    angles = places[:, None] * inverse[None, :]
    return (jnp.cos(angles), jnp.sin(angles))


def rope(pair, cosine, sine):
    lane = lax.broadcasted_iota(jnp.int32, pair.shape, 1)
    former = lane % HD < HD // 2
    turned = jnp.where(
        former, pltpu.roll(pair, 2 * HD - HD // 2, 1), pltpu.roll(pair, HD // 2, 1)
    )
    return pair * cosine + turned * sine


def inverse_rms(values):
    return lax.rsqrt(jnp.mean(values * values, -1, keepdims=True) + EPSILON)


def spec(shape, index=None):
    index = index or (lambda *_: (0,) * len(shape))
    return pl.BlockSpec(shape, index)


def once(shape, index=None):
    index = index or (lambda *_: (0,) * len(shape))
    return pl.BlockSpec(shape, index, pipeline_mode=pl.Buffered(1))


def smem():
    return pl.BlockSpec(memory_space=pltpu.SMEM)


def shape_of(shape, kind):
    return jax.ShapeDtypeStruct(shape, kind)


def call(
    body, grid, in_specs, out_specs, out_shape, scratch, args, flops, moved, limit=56, after=()
):
    count, first = len(after), len(args)

    def ordered(*refs):
        body(*refs[:first], *refs[first + count :])

    return pl.pallas_call(
        ordered,
        grid=grid,
        in_specs=list(in_specs) + [pl.BlockSpec(memory_space=pl.ANY)] * count,
        out_specs=out_specs,
        out_shape=out_shape,
        scratch_shapes=scratch,
        compiler_params=pltpu.CompilerParams(vmem_limit_bytes=limit << 20),
        cost_estimate=pl.CostEstimate(flops=flops, bytes_accessed=moved, transcendentals=0),
    )(*args, *after)


def lanes(index, size):
    return pl.ds(pl.multiple_of(index * size, size), size)


def fill(scratch, shards, rows):
    for j in range(shards.shape[0]):
        scratch[j * rows : (j + 1) * rows, :] = shards[j, :rows, :]


def prepare(index, routes, cotangent, chips):
    micro, rows, width = cotangent.shape
    part = width // chips

    def body(index_ref, routes_ref, cotangent_ref, picks_ref, *messages):
        chip = index_ref[0]
        earlier = lax.broadcasted_iota(jnp.int32, (rows, rows), 0) > lax.broadcasted_iota(
            jnp.int32, (rows, rows), 1
        )
        earlier = jnp.where(earlier, 1.0, 0.0).astype(BF)
        expert = lax.broadcasted_iota(jnp.int32, (rows, 128), 1)
        for m in range(micro):
            chosen = routes_ref[m]
            pick = jnp.zeros((rows, 128), F32)
            for k in range(TOPK):
                pick = pick + jnp.where(chosen[:, k : k + 1] == expert, 1.0, 0.0)
            rank = dot(earlier, pick.astype(BF))
            slot = jnp.where((pick > 0.0) & (rank < CAP), rank, -1.0).T
            picks_ref[m] = pick
            out = messages[m]
            for j in range(chips):
                out[:rows, j * part : (j + 1) * part] = cotangent_ref[m, :, lanes(j ^ chip, part)]
            out[rows:, :] = jnp.concatenate(
                [slot[:16], slot[16:32], jnp.zeros((16, width - 2 * rows), F32)], 1
            ).astype(BF)

    message = (rows + 16, width)
    return call(
        body,
        (1,),
        [smem(), spec(routes.shape), spec(cotangent.shape)],
        [spec((micro, rows, 128))] + [spec(message)] * micro,
        [shape_of((micro, rows, 128), F32)] + [shape_of(message, BF)] * micro,
        [],
        (index, routes, cotangent),
        1 << 26,
        4 << 20,
    )


def project(tokens, first, gain, cosine, sine, after=()):
    micro, rows, width = tokens.shape
    shard = width // first.shape[0]
    columns = first.shape[2]
    queries, keys = H * HD, KVH * HD

    def body(tokens_ref, first_ref, gain_ref, cosine_ref, sine_ref, normed_ref, query_ref, *rest):
        kv_refs, weight = rest[:micro], rest[micro]
        fill(weight, first_ref, shard)
        cos, sin = cosine_ref[...], sine_ref[...]
        for m in range(micro):
            values = tokens_ref[m].astype(F32)
            normed = (values * inverse_rms(values) * gain_ref[...]).astype(BF)
            normed_ref[m * rows : (m + 1) * rows, :] = normed
            for j in range(queries // 256):
                got = dot(normed, weight[:, j * 256 : (j + 1) * 256])
                for i in range(2):
                    turned = rope(got[:, i * 128 : (i + 1) * 128], cos, sin)
                    at = j * 256 + i * 128
                    query_ref[m, :, at : at + 128] = turned.astype(BF)
            for j in range(keys // 256):
                got = dot(normed, weight[:, queries + j * 256 : queries + (j + 1) * 256])
                for i in range(2):
                    turned = rope(got[:, i * 128 : (i + 1) * 128], cos, sin)
                    at = j * 256 + i * 128
                    kv_refs[m][:, at : at + 128] = turned.astype(BF)
            got = dot(normed, weight[:, queries + keys :])
            kv_refs[m][:, keys:] = got.astype(BF)

    kv = (rows, 2 * keys)
    return call(
        body,
        (1,),
        [spec(a.shape) for a in (tokens, first, gain, cosine, sine)],
        [spec((micro * rows, width)), spec((micro, rows, queries))] + [spec(kv)] * micro,
        [shape_of((micro * rows, width), BF), shape_of((micro, rows, queries), BF)]
        + [shape_of(kv, BF)] * micro,
        [pltpu.VMEM((width, columns), BF)],
        (tokens, first, gain, cosine, sine),
        2 * micro * rows * width * columns,
        12 << 20,
        after=after,
    )


def place_heads(pair, which):
    lane = lax.broadcasted_iota(jnp.int32, pair.shape, 1)
    mine = (lane < HD) if which == 0 else (lane >= HD)
    moved = pltpu.roll(pair, HD, 1)
    both = (pair, moved) if which == 0 else (moved, pair)
    return jnp.concatenate([jnp.where(mine, b, 0.0) for b in both], 0)


def attend(index, query, blocks, after=()):
    rows = query.shape[0]
    count = len(blocks)
    steps = KVH // 2
    width = H * HD

    def body(index_ref, query_ref, *refs):
        key_refs, value_refs = refs[:count], refs[count : 2 * count]
        low_ref, turned_ref, stat_ref = refs[2 * count : 2 * count + 3]
        top, total, mixed = refs[2 * count + 3 :]
        ctx = index_ref[2]
        heads = []
        for a in range(2):
            pair = query_ref[:, a * 128 : (a + 1) * 128].astype(F32) * ATTENTION_MULT
            heads.append(place_heads(pair, a).T.astype(BF))

        def visit(j):
            key, value = key_refs[j][...], value_refs[j][...]
            for a in range(2):
                scores = dot(key, heads[a])
                peak = jnp.max(scores, 0, keepdims=True)
                if j:
                    peak = jnp.maximum(peak, top[a])
                expo = jnp.exp(scores - peak)
                added = jnp.sum(expo, 0, keepdims=True)
                got = dot_tn(value, expo.astype(BF))[a * HD : (a + 1) * HD]
                if j:
                    scale = jnp.exp(top[a] - peak)
                    added = added + total[a] * scale
                    got = got + mixed[a] * scale
                top[a] = peak
                total[a] = added
                mixed[a] = got

        visit(0)
        for j in range(1, count):
            pl.when((ctx ^ j) <= ctx)(lambda j=j: visit(j))
        for a in range(2):
            got = mixed[a] / total[a]
            turned = jnp.concatenate([got[:, :rows], got[:, rows:]], 0)
            turned_ref[a * 128 : (a + 1) * 128, :] = turned
            low_ref[:, a * 128 : (a + 1) * 128] = turned.T.astype(BF)
            stat_ref[0, a : a + 1, :] = top[a] + jnp.log(total[a])

    keys = [spec((rows, 128), lambda i: (0, i))] * count
    values = [spec((rows, 128), lambda i: (0, i + steps))] * count
    return call(
        body,
        (steps,),
        [smem(), spec((rows, 256), lambda i: (0, i))] + keys + values,
        [
            spec((rows, 256), lambda i: (0, i)),
            spec((256, rows), lambda i: (i, 0)),
            spec((1, 2, 2 * rows), lambda i: (i, 0, 0)),
        ],
        [
            shape_of((rows, width), BF),
            shape_of((width, rows), F32),
            shape_of((steps, 2, 2 * rows), F32),
        ],
        [
            pltpu.VMEM((2, 1, 2 * rows), F32),
            pltpu.VMEM((2, 1, 2 * rows), F32),
            pltpu.VMEM((2, HD, 2 * rows), F32),
        ],
        (index, query, *blocks, *blocks),
        8 * rows * rows * count * width,
        6 << 20,
        after=after,
    )


def attend_back(index, query, blocks, attended_grad, attended, stats, cosine, sine, after=()):
    rows = query.shape[0]
    count = len(blocks)
    steps = KVH // 2
    half = HD // 2

    def body(index_ref, query_ref, grad_ref, attended_ref, stat_ref, cosine_ref, sine_ref, *refs):
        key_refs, value_refs = refs[:count], refs[count : 2 * count]
        query_out, kv_out = refs[2 * count], refs[2 * count + 1 : 3 * count + 1]
        (query_sum,) = refs[3 * count + 1 :]
        ctx = index_ref[2]
        step = pl.program_id(0)
        heads, grads, heads_t, grads_t, deltas = [], [], [], [], []
        for a in range(2):
            at = slice(a * 128, (a + 1) * 128)
            placed = place_heads(query_ref[:, at].astype(F32) * ATTENTION_MULT, a)
            heads.append(placed.astype(BF))
            heads_t.append(placed.T.astype(BF))
            pair = grad_ref[:, at].astype(F32)
            placed = place_heads(pair, a)
            grads.append(placed.astype(BF))
            grads_t.append(placed.T.astype(BF))
            product = pair.T * attended_ref[at, :]
            deltas.append(
                jnp.concatenate(
                    [jnp.sum(product[i * HD : (i + 1) * HD], 0, keepdims=True) for i in range(2)], 1
                )
            )

        def visit(j):
            key, value = key_refs[j][...], value_refs[j][...]
            key_sum, value_sum = 0.0, 0.0
            for a in range(2):
                probs = jnp.exp(dot(key, heads_t[a]) - stat_ref[0, a : a + 1, :])
                score_grad = (probs * (dot(value, grads_t[a]) - deltas[a])).astype(BF)
                key_sum = key_sum + dot(score_grad, heads[a])
                value_sum = value_sum + dot(probs.astype(BF), grads[a])
                got = dot_tn(key, score_grad)[a * HD : (a + 1) * HD]
                if j:
                    got = got + query_sum[a]
                query_sum[a] = got
            kv_out[j][:, lanes(step, 128)] = key_sum.astype(BF)
            kv_out[j][:, lanes(step + steps, 128)] = value_sum.astype(BF)

        visit(0)
        for j in range(1, count):
            reach = (ctx ^ j) <= ctx
            pl.when(reach)(lambda j=j: visit(j))

            @pl.when(jnp.logical_not(reach) & (step == 0))
            def _(j=j):
                kv_out[j][...] = jnp.zeros_like(kv_out[j])

        cos, sin = cosine_ref[...], sine_ref[...]
        for a in range(2):
            got = query_sum[a] * ATTENTION_MULT
            pieces = []
            for i in range(2):
                former = got[:half, i * rows : (i + 1) * rows]
                latter = got[half:, i * rows : (i + 1) * rows]
                pieces += [former * cos + latter * sin, latter * cos - former * sin]
            query_out[:, a * 128 : (a + 1) * 128] = jnp.concatenate(pieces, 0).T.astype(BF)

    wide = spec((rows, 256), lambda i: (0, i))
    keys = [spec((rows, 128), lambda i: (0, i))] * count
    values = [spec((rows, 128), lambda i: (0, i + steps))] * count
    kv = (rows, 2 * KVH * HD)
    return call(
        body,
        (steps,),
        [
            smem(),
            wide,
            wide,
            spec((256, rows), lambda i: (i, 0)),
            spec((1, 2, 2 * rows), lambda i: (i, 0, 0)),
            spec(cosine.shape),
            spec(sine.shape),
        ]
        + keys
        + values,
        [wide] + [spec(kv)] * count,
        [shape_of((rows, H * HD), BF)] + [shape_of(kv, BF)] * count,
        [pltpu.VMEM((2, HD, 2 * rows), F32)],
        (index, query, attended_grad, attended, stats, cosine, sine, *blocks, *blocks),
        20 * rows * rows * count * H * HD,
        8 << 20,
        after=after,
    )


def route(index, attended, tokens, second, gain, router, picks, chips, after=()):
    rows, width = attended.shape
    shard = width // second.shape[0]
    part = width // chips

    def body(
        index_ref, attended_ref, tokens_ref, second_ref, gain_ref, router_ref, picks_ref,
        hidden_ref, moe_ref, probs_ref, message_ref, weight,
    ):
        chip = index_ref[0]
        fill(weight, second_ref, shard)
        hidden = tokens_ref[...].astype(F32) + RESIDUAL_MULT * dot(attended_ref[...], weight[...])
        hidden_ref[...] = hidden
        moe_in = (hidden * inverse_rms(hidden) * gain_ref[...]).astype(BF)
        moe_ref[...] = moe_in
        picked = picks_ref[...] > 0.0
        chosen = jnp.where(picked, dot(moe_in, router_ref[...]), NEGATIVE)
        expo = jnp.where(picked, jnp.exp(chosen - jnp.max(chosen, -1, keepdims=True)), 0.0)
        probs = expo / jnp.sum(expo, -1, keepdims=True)
        probs_ref[...] = probs
        for j in range(chips):
            message_ref[:rows, j * part : (j + 1) * part] = moe_ref[:, lanes(j ^ chip, part)]
        turned = probs.T
        high = turned.astype(BF).astype(F32)
        low = turned - high
        message_ref[rows:, :] = jnp.concatenate(
            [high[:16], high[16:32], low[:16], low[16:32]], 1
        ).astype(BF)

    return call(
        body,
        (1,),
        [smem()] + [spec(a.shape) for a in (attended, tokens, second, gain, router, picks)],
        [spec((rows, width)), spec((rows, width)), spec((rows, 128)), spec((rows + 16, width))],
        [
            shape_of((rows, width), F32),
            shape_of((rows, width), BF),
            shape_of((rows, 128), F32),
            shape_of((rows + 16, width), BF),
        ],
        [pltpu.VMEM((width, width), BF)],
        (index, attended, tokens, second, gain, router, picks),
        2 * rows * width * width,
        6 << 20,
        after=after,
    )


def expert_row(ref, start, rows, expert, first):
    table = ref[start : start + 16, pl.ds(pl.multiple_of((expert // 16) * rows + first, rows), rows)]
    table = table.astype(F32)
    line = lax.broadcasted_iota(jnp.int32, table.shape, 0) == expert % 16
    return jnp.sum(jnp.where(line, table, 0.0), 0, keepdims=True)


def slots_of(row):
    slot = lax.broadcasted_iota(jnp.int32, (CAP, row.shape[1]), 0).astype(F32)
    return jnp.where(slot == row, 1.0, 0.0)


def experts(index, offset, token_blocks, grad_blocks, gate_up, down, after=()):
    runs = len(token_blocks)
    rows, width = token_blocks[0].shape[0] - 16, token_blocks[0].shape[1]
    count = gate_up[0].shape[0]
    slots = runs * CAP
    part = width // len(gate_up) if len(gate_up) != 5 else width // 4
    pieces = len(gate_up)

    def body(index_ref, *refs):
        tokens_in, grads_in = refs[:runs], refs[runs : 2 * runs]
        at = 2 * runs
        gate_up_in, down_in = refs[at : at + pieces], refs[at + pieces : at + 2 * pieces]
        at += 2 * pieces
        received_ref, pair_ref, inner_ref, hidden_ref, out_ref, back_ref, sens_ref = refs[at : at + 7]
        received, grads, weights, wide, deep = refs[at + 7 :]
        step = pl.program_id(0)

        @pl.when(step == 0)
        def _():
            for k in range(0, runs, 2):
                found = []
                for r in (k, k + 1):
                    takes, probs = [], []
                    for i in range(count):
                        expert = index_ref[3] + offset + i
                        take = slots_of(expert_row(grads_in[r], rows, rows, expert, 0))
                        prob = expert_row(tokens_in[r], rows, rows, expert, 0) + expert_row(
                            tokens_in[r], rows, rows, expert, 2 * rows
                        )
                        takes.append(take)
                        probs.append(jnp.sum(take * prob, 1, keepdims=True))
                    take = jnp.concatenate(takes, 0).astype(BF)
                    found.append(
                        (dot(take, tokens_in[r][:rows, :]), dot(take, grads_in[r][:rows, :]), probs)
                    )
                for i in range(count):
                    span = slice(k * CAP, (k + 2) * CAP)
                    pick = slice(i * CAP, (i + 1) * CAP)
                    received[i, span, :] = jnp.concatenate([f[0][pick] for f in found], 0).astype(BF)
                    grads[i, span, :] = jnp.concatenate([f[1][pick] for f in found], 0).astype(BF)
                    prob = jnp.concatenate([f[2][i] for f in found], 0)
                    weights[i, span, :] = jnp.broadcast_to(prob, (2 * CAP, 128))

        if pieces == 5:
            for j in range(3):
                wide[j * part : (j + 1) * part, :] = gate_up_in[j][0]
                deep[:, j * part : (j + 1) * part] = down_in[j][0]
            wide[3 * part : 3 * part + part // 2, :] = gate_up_in[3][0]
            wide[3 * part + part // 2 :, :] = gate_up_in[4][0]
            deep[: FF // 2, 3 * part :] = down_in[3][0]
            deep[FF // 2 :, 3 * part :] = down_in[4][0]
        else:
            for j in range(pieces):
                wide[j * part : (j + 1) * part, :] = gate_up_in[j][0]
                deep[:, j * part : (j + 1) * part] = down_in[j][0]

        rows_in = received[step]
        received_ref[0] = rows_in
        prob = weights[step][:, :1]
        scaled = RESIDUAL_MULT * grads[step].astype(F32)
        pair = (prob * scaled).astype(BF)
        pair_ref[0] = pair
        both = dot(rows_in, wide[...])
        gate_h, up_h = both[:, :FF], both[:, FF:]
        sigma = jax.nn.sigmoid(gate_h)
        silu_gate = gate_h * sigma
        hidden = (silu_gate * up_h).astype(BF)
        hidden_ref[0] = hidden
        inner = dot_nt(pair, deep[...])
        gate_d = (inner * up_h * sigma * (1.0 + gate_h * (1.0 - sigma))).astype(BF)
        up_d = (inner * silu_gate).astype(BF)
        inner_ref[0, :, :FF] = gate_d
        inner_ref[0, :, FF:] = up_d
        out = dot(hidden, deep[...]).astype(BF).astype(F32)
        out_ref[0] = (prob * out).astype(BF)
        sens = jnp.sum(out * scaled, 1, keepdims=True)
        expert = index_ref[3] + offset + step
        for r in range(runs):
            take = slots_of(expert_row(grads_in[r], rows, rows, expert, 0))
            sens_ref[0, r : r + 1, :] = jnp.sum(
                take * sens[r * CAP : (r + 1) * CAP], 0, keepdims=True
            )
        back_ref[0] = dot_nt(inner_ref[0], wide[...]).astype(BF)

    message = (rows + 16, width)
    step = lambda i: (i, 0, 0)
    sizes = [width, width, 2 * FF, FF, width, width]
    return call(
        body,
        (count,),
        [smem()]
        + [once(message)] * (2 * runs)
        + [spec((1,) + a.shape[1:], step) for a in gate_up]
        + [spec((1,) + a.shape[1:], step) for a in down],
        [spec((1, slots, n), step) for n in sizes] + [spec((1, runs, rows), step)],
        [shape_of((count, slots, n), BF) for n in sizes] + [shape_of((count, runs, rows), F32)],
        [
            pltpu.VMEM((count, slots, width), BF),
            pltpu.VMEM((count, slots, width), BF),
            pltpu.VMEM((count, slots, 128), F32),
            pltpu.VMEM((width, 2 * FF), BF),
            pltpu.VMEM((FF, width), BF),
        ],
        (index, *token_blocks, *grad_blocks, *gate_up, *down),
        count * slots * width * FF * 16,
        count * slots * 14 << 10,
        60,
        after,
    )


def grad_cuts(width, deep):
    part, half = width // 4, width // 8
    if not deep:
        def cut(j, lower):
            first = j * part + (half if lower else 0)
            return slice(first, first + half), slice(None)
        own = (slice(0, part), slice(None))
    else:
        def cut(j, lower):
            first = FF // 2 if lower else 0
            return slice(first, first + FF // 2), slice(j * part, (j + 1) * part)
        own = (slice(None), slice(0, part))
    return [
        [cut(1, False), cut(3, False)],
        [cut(2, True), cut(3, True)],
        [own],
        [cut(2, False)],
        [cut(1, True)],
    ]


def expert_grads(parts, after=()):
    count, slots, width = parts[0][0].shape
    full = [(width, 2 * FF), (FF, width)]
    cuts = [grad_cuts(width, deep) for deep in (False, True)]

    def extent(cut, size):
        return [len(range(n)[c]) for c, n in zip(cut, size)]

    shapes = []
    for size, pieces in zip(full, cuts):
        for piece in pieces:
            one = extent(piece[0], size)
            shapes.append((one[0] * len(piece), one[1]))

    def body(*refs):
        ins, outs = refs[: 4 * len(parts)], refs[4 * len(parts) :]
        received, pair, inner, hidden = [
            jnp.concatenate([ins[4 * p + i][0] for p in range(len(parts))], 0) for i in range(4)
        ]
        grads = dot_tn(received, inner).astype(BF), dot_tn(hidden, pair).astype(BF)
        at = 0
        for grad, pieces in zip(grads, cuts):
            for piece in pieces:
                row = 0
                for cut in piece:
                    value = grad[cut]
                    outs[at][0, row : row + value.shape[0], :] = value
                    row += value.shape[0]
                at += 1

    step = lambda i: (i, 0, 0)
    flat = [a for p in parts for a in p]
    got = call(
        body,
        (count,),
        [spec((1,) + a.shape[1:], step) for a in flat],
        [spec((1,) + n, step) for n in shapes],
        [shape_of((count,) + n, BF) for n in shapes],
        [],
        flat,
        len(parts) * count * slots * width * FF * 6,
        len(flat) * count * slots * 2 << 10,
        after=after,
    )
    return got[:5], got[5:]


def reduce_first(pieces):
    send_x, send_y, own, keep_y, keep_x = pieces
    x_own, x_rest = halves(plane_swap(send_x, 2))
    y_own, y_rest = halves(plane_swap(send_y, 4))
    return own, x_own, y_own, add(keep_y, x_rest).astype(BF), add(keep_x, y_rest).astype(BF)


def reduce_last(state):
    own, x_own, y_own, upper, lower = state
    from_y, from_x = plane_swap(upper, 4), plane_swap(lower, 2)
    top, low = halves(own)
    return jnp.concatenate([add(top, x_own) + from_y.astype(F32), add(low, y_own) + from_x.astype(F32)], -2)


def combine(index, grad_blocks, sources, senses=None, after=()):
    runs = len(grad_blocks)
    rows, width = grad_blocks[0].shape[0] - 16, grad_blocks[0].shape[1]
    chunks = len(sources)
    counts = [a.shape[0] for a in sources]
    steps = runs // 2
    total = sum(counts)
    senses = [a.reshape(a.shape[0], steps, 2, rows) for a in senses or ()]
    tall = rows + 16 if senses else rows

    def body(index_ref, *refs):
        slots_in, pairs_in = refs[:runs], refs[runs : runs + chunks]
        sens_in = refs[runs + chunks : runs + chunks + len(senses)]
        mine, *others = refs[runs + chunks + len(senses) :][: 1 + steps]
        table, choice = refs[runs + chunks + len(senses) + 1 + steps :]
        step = pl.program_id(0)
        first = index_ref[3]

        def fetch(k):
            for i in range(total):
                lines = [slots_of(expert_row(slots_in[2 * k + s], 0, rows, first + i, 0)) for s in range(2)]
                zero = jnp.zeros_like(lines[0])
                at = i * 2 * CAP
                choice[at : at + 2 * CAP, :] = jnp.concatenate(
                    [
                        jnp.concatenate([lines[0], zero], 1),
                        jnp.concatenate([zero, lines[1]], 1),
                    ],
                    0,
                ).astype(BF)

        for k in range(steps):
            pl.when(step == k)(lambda k=k: fetch(k))
        flat = jnp.concatenate(
            [a[...].reshape(n * 2 * CAP, width) for a, n in zip(pairs_in, counts)], 0
        )
        got = dot_tn(choice[...], flat).astype(BF)

        def put(s, first_row, last_row, value):
            if s == 0:
                mine[0, first_row:last_row, :] = value
                return
            for k in range(steps):

                @pl.when(step == k)
                def _(k=k):
                    others[k][first_row:last_row, :] = value

        for s in range(2):
            put(s, 0, rows, got[s * rows : (s + 1) * rows])
            if not senses:
                continue
            table[...] = jnp.zeros_like(table)
            i = 0
            for ref, n in zip(sens_in, counts):
                for e in range(n):
                    line = ref[e, 0, s : s + 1, :]
                    high = line.astype(BF).astype(F32)
                    expert = first + i
                    lane = (expert // 16) * rows
                    for value, base in ((high, 0), (line - high, 2 * rows)):
                        table[
                            pl.ds(expert % 16, 1), pl.ds(pl.multiple_of(lane + base, rows), rows)
                        ] = value
                    i += 1
            put(s, rows, rows + 16, table[...].astype(BF))

    return call(
        body,
        (steps,),
        [smem()]
        + [once((16, width), lambda k: (rows // 16, 0))] * runs
        + [spec((n, 2 * CAP, width), lambda k: (0, k, 0)) for n in counts]
        + [spec((a.shape[0], 1, 2, rows), lambda k: (0, k, 0, 0)) for a in senses],
        [spec((1, tall, width), lambda k: (k, 0, 0))] + [spec((tall, width))] * steps,
        [shape_of((steps, tall, width), BF)] + [shape_of((tall, width), BF)] * steps,
        [pltpu.VMEM((16, width), F32), pltpu.VMEM((total * 2 * CAP, 2 * rows), BF)],
        (index, *grad_blocks, *sources, *senses),
        4 * runs * total * CAP * rows * width,
        total * runs * CAP * width * 2,
        after=after,
    )


def hidden_back(
    index, total, hidden, gain, probs, cotangent, router, second, chips, after=()
):
    rows, width = hidden.shape
    shard = width // second.shape[0]
    part = width // chips

    def body(
        index_ref, total_ref, hidden_ref, gain_ref, probs_ref, cotangent_ref, router_ref, second_ref,
        hidden_grad_ref, branch_ref, attended_ref, logit_ref, norm_ref, weight,
    ):
        chip = index_ref[0]
        fill(weight, second_ref, shard)
        tail = total_ref[rows:, :].astype(F32)
        tail = tail[:, : 2 * rows] + tail[:, 2 * rows :]
        sens = jnp.concatenate(
            [tail[:, :rows], tail[:, rows:], jnp.zeros((128 - EXPERTS, rows), F32)], 0
        ).T
        probs = probs_ref[...]
        logit_grad = probs * (sens - jnp.sum(probs * sens, -1, keepdims=True))
        logit_grad = logit_grad.astype(BF)
        logit_ref[...] = logit_grad
        moved = jnp.concatenate(
            [total_ref[:rows, lanes(j ^ chip, part)] for j in range(chips)], 1
        ).astype(F32)
        moe_grad = moved + dot_nt(logit_grad, router_ref[...])
        hidden = hidden_ref[...]
        factor = inverse_rms(hidden)
        normed = hidden * factor
        norm_ref[...] = jnp.sum(moe_grad * normed, 0, keepdims=True)
        scaled = moe_grad * gain_ref[...]
        hidden_grad = cotangent_ref[...].astype(F32) + factor * (
            scaled - normed * jnp.mean(scaled * normed, -1, keepdims=True)
        )
        hidden_grad_ref[...] = hidden_grad
        branch = (RESIDUAL_MULT * hidden_grad).astype(BF)
        branch_ref[...] = branch
        attended_ref[...] = dot_nt(branch, weight[...]).astype(BF)

    args = (index, total, hidden, gain, probs, cotangent, router, second)
    return call(
        body,
        (1,),
        [smem()] + [spec(a.shape) for a in args[1:]],
        [spec((rows, width))] * 3 + [spec((rows, 128)), spec((1, width))],
        [
            shape_of((rows, width), F32),
            shape_of((rows, width), BF),
            shape_of((rows, width), BF),
            shape_of((rows, 128), BF),
            shape_of((1, width), F32),
        ],
        [pltpu.VMEM((width, width), BF)],
        args,
        2 * rows * width * width,
        8 << 20,
        after=after,
    )


def input_back(query_grad, kv_parts, tokens, first, gain, hidden_grad, cosine, sine, after=()):
    rows, width = tokens.shape
    shard = width // first.shape[0]
    columns = first.shape[2]
    queries, keys = H * HD, KVH * HD
    count = len(kv_parts)

    def body(query_ref, tokens_ref, first_ref, gain_ref, hidden_ref, cosine_ref, sine_ref, *refs):
        kv_refs = refs[:count]
        input_ref, low_ref, norm_ref, weight = refs[count:]
        fill(weight, first_ref, shard)
        cos, sin = cosine_ref[...], -sine_ref[...]
        low_ref[:, :queries] = query_ref[...]
        key = sum(r[:, :keys].astype(F32) for r in kv_refs)
        for j in range(keys // 128):
            turned = rope(key[:, j * 128 : (j + 1) * 128], cos, sin)
            low_ref[:, queries + j * 128 : queries + (j + 1) * 128] = turned.astype(BF)
        value = sum(r[:, keys:].astype(F32) for r in kv_refs)
        low_ref[:, queries + keys :] = value.astype(BF)
        sens = dot_nt(low_ref[...], weight[...])
        values = tokens_ref[...].astype(F32)
        factor = inverse_rms(values)
        normed = values * factor
        norm_ref[...] = jnp.sum(sens * normed, 0, keepdims=True)
        scaled = sens * gain_ref[...]
        input_ref[...] = (
            hidden_ref[...]
            + factor * (scaled - normed * jnp.mean(scaled * normed, -1, keepdims=True))
        ).astype(BF)

    args = (query_grad, tokens, first, gain, hidden_grad, cosine, sine, *kv_parts)
    return call(
        body,
        (1,),
        [spec(a.shape) for a in args],
        [spec((rows, width)), spec((rows, columns)), spec((1, width))],
        [shape_of((rows, width), BF), shape_of((rows, columns), BF), shape_of((1, width), F32)],
        [pltpu.VMEM((width, columns), BF)],
        args,
        2 * rows * width * columns,
        8 << 20,
        after=after,
    )


def on_device(
    tokens,
    routes,
    cotangent,
    norm_one,
    norm_two,
    w_query,
    w_key,
    w_value,
    w_out,
    w_router,
    w_gate,
    w_up,
    w_down,
):
    micro_count, _, rows, width = tokens.shape
    tokens, routes, cotangent = tokens[:, 0], routes[:, 0], cotangent[:, 0]
    local_experts, shard = w_gate.shape[0], w_gate.shape[1]
    core_experts = local_experts // 2
    ctx_count, exp_count = lax.axis_size("ctx"), lax.axis_size("exp")
    plane = lax.axis_size("dp") * ctx_count
    chips = plane // 2
    ctx = lax.axis_index("ctx")
    place = lax.axis_index("dp") * ctx_count + ctx
    chip, core = place // 2, place % 2
    first_expert = lax.axis_index("exp") * local_experts + core * core_experts
    index = jnp.stack([chip, core, ctx, first_expert]).astype(jnp.int32)
    micros = range(micro_count)

    cosine, sine = rotation(ctx * rows, rows)
    cosine_t, sine_t = cosine.T, sine.T
    cosine_w = jnp.tile(cosine, (1, 4))
    sine_w = jnp.concatenate([-sine, sine, -sine, sine], 1)

    gains = jnp.concatenate([norm_one, norm_two])[None, :]
    gains = jnp.pad(gains, ((0, 15), (0, w_query.shape[1] * 2 - gains.shape[1])))
    first_set = jnp.concatenate([jnp.concatenate([w_query, w_key, w_value], 1), gains], 0)
    router_rows = w_router.reshape(-1, width)
    router_count = router_rows.shape[0]
    router_rows = jnp.pad(router_rows, ((0, 16 - router_count), (0, 0)))
    second_set = jnp.concatenate([w_out, router_rows], 0)
    first = lax.all_gather(first_set, PLANE)
    second = lax.all_gather(second_set, PLANE)
    gain_one = first[:, shard, :shard].reshape(1, width).astype(F32)
    gain_two = first[:, shard, shard : 2 * shard].reshape(1, width).astype(F32)
    router = second[:, shard : shard + router_count].reshape(width, EXPERTS)
    router = jnp.pad(router, ((0, 0), (0, 128 - EXPERTS)))

    def later(array, *others):
        return lax.optimization_barrier((array,) + others)[0]

    class Ring:
        def __init__(self, message):
            self.blocks, self.siblings = [message], [sibling(message)]

        def step(self):
            self.blocks.append(ring_step(self.blocks[-1]))
            self.siblings.append(sibling(self.blocks[-1]))
            return self.blocks[-1]

        def runs(self):
            while len(self.blocks) < exp_count:
                self.step()
            return [b for pair in zip(self.blocks, self.siblings) for b in pair]

    class Home:
        def __init__(self, mine, others):
            self.got = [sibling(o) for o in others[1:] + others[:1]]
            self.got = self.got[-1:] + self.got[:-1]
            self.mine = mine
            self.at = 1
            self.total = add(mine[1], self.got[1]).astype(BF)

        def step(self):
            self.at += 1
            k = self.at % exp_count
            moved = ring_step(self.total).astype(F32)
            self.total = (moved + add(self.mine[k], self.got[k])).astype(BF)
            return self.total

        def end(self):
            while self.at < exp_count:
                self.step()
            return self.total

    def swap_in(array, axis):
        mine = lax.dynamic_slice_in_dim(array, core * core_experts, core_experts, 0)
        other = lax.dynamic_slice_in_dim(array, (1 - core) * core_experts, core_experts, 0)
        got = sibling(other)
        pair = [jnp.where(core == 0, mine, got), jnp.where(core == 0, got, mine)]
        return jnp.concatenate(pair, axis)

    def swap_out(array, axis):
        half = array.shape[axis] // 2
        mine = lax.dynamic_slice_in_dim(array, core * half, half, axis)
        other = lax.dynamic_slice_in_dim(array, (1 - core) * half, half, axis)
        got = sibling(other.astype(BF)).astype(F32)
        pair = [jnp.where(core == 0, mine, got), jnp.where(core == 0, got, mine)]
        return jnp.concatenate(pair, 0)

    def run_attention(m, after=()):
        low, turned, stats = attend(index, query[m], kv_blocks[m], after)
        return low, turned, stats

    def run_route(m, low, after=()):
        return route(
            index, low, tokens[m], second, gain_two, router, picks[m], chips, after
        )

    def run_hidden_back(m, in_total, after=()):
        return hidden_back(
            index, in_total, hidden[m], gain_two, probs[m], cotangent[m], router, second, chips, after
        )

    def run_attend_back(m, attended_grad, after=()):
        return attend_back(
            index, query[m], kv_blocks[m], attended_grad, turned[m], stats[m], cosine_t, sine_t, after
        )

    def run_input_back(m, query_grad, kv_parts, hidden_grad, after=()):
        return input_back(
            query_grad, kv_parts, tokens[m], first, gain_one, hidden_grad, cosine_w, sine_w, after
        )

    def finish_output(m, total):
        rows_out = reorder(total, chips, chip, 1).astype(F32)
        return (hidden[m] + RESIDUAL_MULT * rows_out).astype(BF)

    picks, *messages = prepare(index, routes, cotangent, chips)
    g_rings = [Ring(message) for message in messages]
    gate_up_own = swap_in(jnp.concatenate([w_gate, w_up], 2), 1)
    down_own = swap_in(w_down, 2)
    attended_low, turned, stats, hidden, moe_in, probs = [[None] * micro_count for _ in range(6)]
    backs, outputs = [None] * micro_count, [None] * micro_count

    if chips == 4 and exp_count == 4 and ctx_count == 4 and micro_count == 2 and core_experts % 2 == 0:
        half = core_experts // 2

        class Weights:
            def __init__(self, c, *after):
                self.near = []
                for array in (gate_up_own, down_own):
                    own = later(array[c * half : (c + 1) * half], *after)
                    self.near.append((own, plane_swap(own, 2), plane_swap(own, 4)))

            def hand_on(self):
                self.parts = [(halves(x)[0], halves(y)[1]) for _, x, y in self.near]
                return tuple(a for pair in self.parts for a in pair)

            def full(self):
                return [
                    near + (plane_swap(a, 4), plane_swap(b, 2))
                    for near, (a, b) in zip(self.near, self.parts)
                ]

        def one_experts(c, m, full, after):
            return experts(index, c * half, x_rings[m].runs(), g_rings[m].runs(), *full, after=after)

        def gather_near(kv):
            near = lax.ppermute(kv, "ctx", [(0, 1), (2, 3)])
            along = lax.ppermute(kv, "ctx", [(0, 2), (1, 3)])
            far = lax.ppermute(along, "ctx", [(2, 3), (3, 2)])
            return [kv, near, along, far]

        g_steps = [ring.step() for ring in g_rings]
        normed_in, query, *kv_own = project(tokens, first, gain_one, cosine_w, sine_w, g_steps)
        g_steps = [ring.step() for ring in g_rings]
        kv_blocks = [gather_near(kv) for kv in kv_own]
        early = Weights(0, first)
        x_rings = [None, None]
        attended_low[0], turned[0], stats[0] = run_attention(0, g_steps)
        hidden[0], moe_in[0], probs[0], message = run_route(0, attended_low[0])
        g_steps = [ring.step() for ring in g_rings]
        x_rings[0] = Ring(message)
        attended_low[1], turned[1], stats[1] = run_attention(1, early.hand_on() + (message,))
        late = Weights(1, message)
        hidden[1], moe_in[1], probs[1], message = run_route(1, attended_low[1], g_steps)
        x_rings[1] = Ring(message)
        x_rings[0].step()
        x_rings[0].step()
        x_rings[1].step()
        early_full = early.full()
        got = {}
        got[0, 0] = one_experts(0, 0, early_full, late.hand_on() + (x_rings[1].step(),))
        late_full = late.full()
        got[1, 0] = one_experts(1, 0, late_full, (got[0, 0][4], x_rings[1].step()))

        def run_combine(m, kind, after):
            pieces = [got[c, m][4:] for c in range(2)]
            senses = [p[2] for p in pieces] if kind else None
            sources = [p[kind] for p in pieces]
            mine, *others = combine(index, g_rings[m].runs(), sources, senses, after)
            return mine, others

        mine, others = run_combine(0, 1, (got[1, 0][4],))
        in_home = [Home(mine, others)]
        got[0, 1] = one_experts(0, 1, early_full, (in_home[0].total,))
        got[1, 1] = one_experts(1, 1, late_full, (got[0, 1][4], in_home[0].step()))
        mine, others = run_combine(1, 1, (got[1, 1][4], in_home[0].step()))
        in_home.append(Home(mine, others))
        in_home[0].end()
        grads = [expert_grads([got[0, m][:4] for m in micros], (in_home[1].total,))]
        reducing = [[reduce_first(p) for p in grads[0]]]
        grads.append(
            expert_grads([got[1, m][:4] for m in micros], (grads[0][0][0], in_home[0].total))
        )
        reducing.append([reduce_first(p) for p in grads[1]])
        step_one = in_home[1].step()
        hidden_grad, branch, attended_grad, logit, norm_two_0 = run_hidden_back(
            0, in_home[0].total, (grads[1][0][0], step_one)
        )
        hidden_grads, branches, logits = [hidden_grad], [branch], [logit]
        query_grad, *parts = run_attend_back(0, attended_grad, (in_home[1].step(),))
        query_grads, kv_parts = [query_grad], [parts]

        def send_back(parts):
            far = lax.ppermute(parts[3], "ctx", [(2, 3), (3, 2)])
            return add(parts[2], far).astype(BF)

        def arrive_back(parts, along):
            near = lax.ppermute(parts[1], "ctx", [(1, 0), (3, 2)])
            return [parts[0], near, lax.ppermute(along, "ctx", [(2, 0), (3, 1)])]

        mine, others = run_combine(0, 0, (query_grad,))
        out_home = [Home(mine, others)]
        along = [send_back(parts)]
        first_adds = [a for r in reducing[0] for a in r[3:]]
        hidden_grad, branch, attended_grad, logit, norm_two_1 = run_hidden_back(
            1, in_home[1].end(), (mine, along[0], *first_adds)
        )
        hidden_grads.append(hidden_grad)
        branches.append(branch)
        logits.append(logit)
        query_grad, *parts = run_attend_back(1, attended_grad, (out_home[0].total,))
        query_grads.append(query_grad)
        kv_parts.append(parts)
        along.append(send_back(parts))
        mine, others = run_combine(1, 0, (query_grad, out_home[0].step()))
        out_home.append(Home(mine, others))
        backs[0] = run_input_back(
            0, query_grads[0], arrive_back(kv_parts[0], along[0]), hidden_grads[0], (mine, along[1])
        )
        second_adds = [a for r in reducing[1] for a in r[3:]]
        backs[1] = run_input_back(
            1,
            query_grads[1],
            arrive_back(kv_parts[1], along[1]),
            hidden_grads[1],
            (backs[0][1], out_home[1].total, out_home[0].step(), *second_adds),
        )
        norm_two_sum = norm_two_0 + norm_two_1
        for m in micros:
            outputs[m] = finish_output(m, out_home[m].end())
        gate_up_sum, down_sum = [
            swap_out(jnp.concatenate([reduce_last(r[i]) for r in reducing], 0), 1 + i)
            for i in range(2)
        ]
    else:
        full = [gather_chips(later(a, first)) for a in (gate_up_own, down_own)]
        normed_in, query, *kv_own = project(tokens, first, gain_one, cosine_w, sine_w)
        kv_blocks, last = [None] * micro_count, first
        branches, logits = [None] * micro_count, [None] * micro_count
        norm_two_sum, gate_up_grad, down_grad = 0.0, 0.0, 0.0
        group = min(exp_count, 4)
        for m in micros:
            kv_blocks[m] = gather_ctx(later(kv_own[m], last))
            attended_low[m], turned[m], stats[m] = run_attention(m)
            hidden[m], moe_in[m], probs[m], message = run_route(m, attended_low[m])
            x_runs, g_runs = Ring(message).runs(), g_rings[m].runs()
            mines, others = [[], []], [[], []]
            for g in range(0, exp_count, group):
                span = slice(2 * g, 2 * (g + group))
                after = (last,)
                *kept, out, back, sens = experts(
                    index, 0, x_runs[span], g_runs[span], *full, after=after
                )
                gate_up_grad += jnp.einsum(
                    "esd,esf->edf", kept[0], kept[2], preferred_element_type=F32
                )
                down_grad += jnp.einsum("esf,esd->efd", kept[3], kept[1], preferred_element_type=F32)
                for i, source in enumerate((out, back)):
                    mine, *other = combine(
                        index, g_runs[span], [source], [sens] if i else None, after
                    )
                    mines[i] += [mine[k] for k in range(group)]
                    others[i] += other
                last = mine
            in_total = Home(mines[1], others[1]).end()
            outputs[m] = finish_output(m, Home(mines[0], others[0]).end())
            last = outputs[m]
            hidden_grad, branches[m], attended_grad, logits[m], norm = run_hidden_back(m, in_total)
            norm_two_sum += norm
            query_grad, *parts = run_attend_back(m, attended_grad)
            kv_sum = reduce_ctx(parts).astype(BF)
            backs[m] = run_input_back(m, query_grad, [kv_sum], hidden_grad)
        gate_up_sum = jnp.split(gate_up_grad.astype(BF), chips, 1)
        down_sum = jnp.split(down_grad.astype(BF), chips, 2)
        gate_up_sum = swap_out(reduce_chips(gate_up_sum), 1)
        down_sum = swap_out(reduce_chips(down_sum), 2)

    input_grads = [b[0] for b in backs]
    lows = [b[1] for b in backs]
    norm_one_sum = sum(b[2] for b in backs)

    def stack_rows(parts):
        return jnp.concatenate(parts, 0)

    attended_rows = stack_rows(attended_low)
    moe_rows = stack_rows(moe_in)
    second_sum = dot_tn(attended_rows, stack_rows(branches)).astype(BF)
    router_sum = dot_tn(moe_rows, stack_rows(logits))[:, :EXPERTS]
    first_sum = dot_tn(normed_in, stack_rows(lows)).astype(BF)
    small = jnp.concatenate([norm_one_sum.T, norm_two_sum.T, router_sum], 1).astype(BF)
    small = jnp.pad(small, ((0, 0), (0, 128 - small.shape[1])))
    packed = jnp.concatenate([first_sum, second_sum, small], 1)
    total = lax.psum_scatter(packed, PLANE, scatter_dimension=0, tiled=True)
    total = lax.psum(total, "exp").astype(F32)
    cuts = [H * HD, (H + KVH) * HD, (H + 2 * KVH) * HD, (H + 2 * KVH) * HD + width]
    query_grad, key_grad, value_grad, out_grad, small = jnp.split(total, cuts, 1)
    return (
        jnp.stack(outputs)[:, None],
        jnp.stack(input_grads)[:, None],
        small[:, 0],
        small[:, 1],
        query_grad,
        key_grad,
        value_grad,
        out_grad,
        small[:, 2 : 2 + EXPERTS],
        gate_up_sum[..., :FF],
        gate_up_sum[..., FF:],
        down_sum,
    )


def solution(mesh):
    rows = P(None, ("dp", "exp"), "ctx", None)
    row_shard = P(PLANE, None)
    return jax.shard_map(
        on_device,
        mesh=mesh,
        in_specs=(
            rows,
            rows,
            rows,
            P(PLANE),
            P(PLANE),
            row_shard,
            row_shard,
            row_shard,
            row_shard,
            row_shard,
            P("exp", PLANE, None),
            P("exp", PLANE, None),
            P("exp", None, PLANE),
        ),
        out_specs=(
            rows,
            rows,
            P(PLANE),
            P(PLANE),
            row_shard,
            row_shard,
            row_shard,
            row_shard,
            row_shard,
            P("exp", PLANE, None),
            P("exp", PLANE, None),
            P("exp", None, PLANE),
        ),
        check_vma=False,
    )
```

time: 1970 us -> 709 us (0.36)
  waiting for transfers between devices: 1210 us -> 268 us
  matrix products: 256 us -> 7.87 us
  local copies, waits for them, and re-layouts: 249 us -> 33.3 us
  Pallas kernels: 0 us -> 197 us
  blocking collectives: 74.1 us -> 0 us
  starting transfers between devices: 42.5 us -> 112 us
  other arithmetic: 113 us -> 71.5 us
    all_to_all x8 -> x0, waiting for transfers between devices: 660 us -> none  [the longest x2 199 us: on_device(): lax.all_to_all(send_grad, 'exp', split_axis=0, concat_axis=1, tiled=True)]
    reduce_scatter x10 -> x1, waiting for transfers between devices: 411 us -> 0.01 us  [on_device(): total = lax.psum_scatter(packed, PLANE, scatter_dimension=0, tiled=True)]
    dot_general x62 -> x3, matrix products: 256 us -> 7.87 us  [dot_tn(): lax.dot_general(left, right, (((0,), (0,)), ((), ())), preferred_element_...]
    ppermute x0 -> x104, waiting for transfers between devices: none -> 235 us  [the longest x24 108 us: ring_step(): lax.ppermute(array, 'exp', [(i, (i + 1) % count) for i in range(count)])]
    pallas_call x0 -> x22, Pallas kernels: none -> 197 us  [call(): pl.pallas_call(ordered, grid=grid, in_specs=list(in_specs) + [pl.BlockSpe...]
    all_gather x11 -> x2, waiting for transfers between devices: 120 us -> 0.01 us  [the longest x1 0.01 us: on_device(): second = lax.all_gather(second_set, PLANE)]
    ppermute x0 -> x104, starting transfers between devices: none -> 112 us  [the longest x68 59.8 us: plane_swap(): return lax.ppermute(array, PLANE, [(i, i ^ mask) for i in range(count)])]
    gather x4 -> x0, local copies, waits for them, and re-layouts: 56.5 us -> none  [the longest x2 28.4 us: on_device(): back_table[slot_index].reshape(row_count, TOPK, model_width)]
  transfers between devices with their start and end apart: 32 -> 108, of which waited for: 26 -> 34; matrix products, arithmetic and copies ran while one was open for 21% -> 13% of each run, Pallas kernels for 0% -> 26%
where the time goes in v1:
time: 709 us; the launch traced here: 704 us
  waiting for transfers between devices  268 us (38%)
  Pallas kernels  197 us (28%)
  starting transfers between devices  112 us (16%)
  other arithmetic  71.5 us (10%)
  local copies, waits for them, and re-layouts  33.3 us (5%)
  between operations  15.6 us (2%)
  matrix products  7.87 us (1%)
    pallas_call x22, Pallas kernels, call(): pl.pallas_call(ordered, grid=grid, in_specs=list(in_specs) + [pl.BlockSpe...  197 us
    ppermute x24, waiting for transfers between devices, ring_step(): lax.ppermute(array, 'exp', [(i, (i + 1) % count) for i in range(count)])  108 us
    ppermute x68, waiting for transfers between devices, plane_swap(): return lax.ppermute(array, PLANE, [(i, i ^ mask) for i in range(count)])  98.1 us
    ppermute x68, starting transfers between devices, plane_swap(): return lax.ppermute(array, PLANE, [(i, i ^ mask) for i in range(count)])  59.8 us
    psum x1, waiting for transfers between devices, on_device(): total = lax.psum(total, 'exp').astype(F32)  32.5 us
    ppermute x24, starting transfers between devices, ring_step(): lax.ppermute(array, 'exp', [(i, (i + 1) % count) for i in range(count)])  19.9 us
    convert_element_type x12, other arithmetic, step(): self.total = (moved + add(self.mine[k], self.got[k])).astype(BF)  18.7 us
    ppermute x2, waiting for transfers between devices, arrive_back(): return [parts[0], near, lax.ppermute(along, 'ctx', [(2, 0), (3, 1)])]  14.5 us
  transfers between devices with their start and end apart: 108, of which 34 were waited for; matrix products, arithmetic and copies ran while one was open for 13% of the time, Pallas kernels for 26%

profile of v1, /device:TPU:0, one launch (start us, length us, event | category | flops | bytes accessed | tf_op | source)
XLA Modules:
  0.0 704.5 jit_solution(11176046120133869942)
XLA Ops:
  27.4 8.8 %collective-permute-done.refs_5_.refs_11_.refs_3_ = bf16[272,1024]{1,0:T(8,128)(2,1)} collective-permute-done((bf16[272,1024]{1,0:T(8,128)(2,1)}, bf16[272,1024]{1,0:T(8,128)(2,1)}, u32[]{:S(2)}, u32[]{:S(2)}) %collective-permute-start) | collective-permute-done | bytes 557088 | tf_op jit(solution)/shard_map/ppermute | solution.py:157
  38.4 9.6 %collective-permute-done.1.refs_6_.refs_11_.refs_3_ = bf16[272,1024]{1,0:T(8,128)(2,1)S(1)} collective-permute-done((bf16[272,1024]{1,0:T(8,128)(2,1)}, bf16[272,1024]{1,0:T(8,128)(2,1)S(1)}, u32[]{:S(2)}, u32[]{:S(2)}) %collective-permute-start.1) | collective-permute-done | bytes 557088 | tf_op jit(solution)/shard_map/ppermute | solution.py:157
  50.5 9.6 %collective-permute-done.5.refs_10_.refs_13_.refs_5_ = bf16[272,1024]{1,0:T(8,128)(2,1)} collective-permute-done((bf16[272,1024]{1,0:T(8,128)(2,1)}, bf16[272,1024]{1,0:T(8,128)(2,1)}, u32[]{:S(2)}, u32[]{:S(2)}) %collective-permute-start.5) | collective-permute-done | bytes 557088 | tf_op jit(solution)/shard_map/ppermute | solution.py:157
  61.5 6.4 shard_map.221
  67.9 4.1 collective-permute-done.6.refs_11_.refs_13_.refs_5_
  72.0 4.4 collective-permute-start.3
  77.6 6.3 collective-permute-done.10.refs_7_.refs_15_
  110.9 6.5 shard_map.222
  117.4 4.1 shard_map.223
  121.5 14.1 %collective-permute-done.34.refs_4_.refs_8_.refs_9_.refs_13_ = bf16[256,1024]{1,0:T(8,128)(2,1)S(1)} collective-permute-done((bf16[256,1024]{1,0:T(8,128)(2,1)}, bf16[256,1024]{1,0:T(8,128)(2,1)S(1)}, u32[]{:S(2)}, u32[]{:S(2)}) %collective-permute-start.34) | collective-permute-done | bytes 524320 | tf_op jit(solution)/shard_map/ppermute | solution.py:1101
  137.4 12.7 %collective-permute-start.35 = (bf16[256,1024]{1,0:T(8,128)(2,1)S(1)}, bf16[256,1024]{1,0:T(8,128)(2,1)S(1)}, u32[]{:S(2)}, u32[]{:S(2)}) collective-permute-start(bf16[256,1024]{1,0:T(8,128)(2,1)S(1)} %collective-permute-done.34.refs_4_.refs_8_.refs_9_.refs_13_), channel_id=1, source_target_pairs={{8,12},{12,8},{9,13},{13,9},{10,14},{14,10},{11,15},{15,11},{24,28... | collective-permute-start | bytes 1572872 | tf_op jit(solution)/shard_map/ppermute | solution.py:1102
  159.7 9.7 %collective-permute-done.27.refs_25_ = bf16[2,256,256]{2,1,0:T(8,128)(2,1)S(1)} collective-permute-done((bf16[2,256,256]{2,1,0:T(8,128)(2,1)S(1)}, bf16[2,256,256]{2,1,0:T(8,128)(2,1)S(1)}, u32[]{:S(2)}, u32[]{:S(2)}) %collective-permute-start.27) | collective-permute-done | bytes 262176 | tf_op jit(solution)/shard_map/ppermute | solution.py:61
  169.4 5.4 collective-permute-start.23
  178.5 6.5 shard_map.224
  185.0 4.2 shard_map.225
  192.2 6.6 collective-permute-done.31.refs_23_
  200.3 11.9 %collective-permute-done.32.refs_24_ = bf16[2,512,256]{2,1,0:T(8,128)(2,1)S(1)} collective-permute-done((bf16[2,512,256]{2,1,0:T(8,128)(2,1)S(1)}, bf16[2,512,256]{2,1,0:T(8,128)(2,1)S(1)}, u32[]{:S(2)}, u32[]{:S(2)}) %collective-permute-start.32) | collective-permute-done | bytes 524320 | tf_op jit(solution)/shard_map/ppermute | solution.py:61
  212.7 7.6 %collective-permute-done.29.refs_18_ = bf16[2,256,1024]{2,1,0:T(8,128)(2,1)S(1)} collective-permute-done((bf16[2,256,1024]{2,1,0:T(8,128)(2,1)S(1)}, bf16[2,256,1024]{2,1,0:T(8,128)(2,1)S(1)}, u32[]{:S(2)}, u32[]{:S(2)}) %collective-permute-start.29) | collective-permute-done | bytes 1048608 | tf_op jit(solution)/shard_map/ppermute | solution.py:61
  226.7 9.3 %collective-permute-done.38.refs_31_.refs_5_ = bf16[272,1024]{1,0:T(8,128)(2,1)} collective-permute-done((bf16[272,1024]{1,0:T(8,128)(2,1)S(1)}, bf16[272,1024]{1,0:T(8,128)(2,1)}, u32[]{:S(2)}, u32[]{:S(2)}) %collective-permute-start.38) | collective-permute-done | bytes 557088 | tf_op jit(solution)/shard_map/ppermute | solution.py:157
  239.8 16.7 %shard_map.226 = (bf16[2,576,1024]{2,1,0:T(8,128)(2,1)}, bf16[2,576,1024]{2,1,0:T(8,128)(2,1)}, bf16[2,576,1024]{2,1,0:T(8,128)(2,1)}, bf16[2,576,512]{2,1,0:T(8...) custom-call(s32[4]{0:T(128)} %pad_add_fusion.refs_0_, ...), custom_call_target="tpu_custom_call" | custom-call | flops 9663676416 | bytes 16515072 | tf_op jit(solution)/shard_map/pallas_call | solution.py:222
  258.4 16.6 %shard_map.227 = (bf16[2,576,1024]{2,1,0:T(8,128)(2,1)}, bf16[2,576,1024]{2,1,0:T(8,128)(2,1)}, bf16[2,576,1024]{2,1,0:T(8,128)(2,1)}, bf16[2,576,512]{2,1,0:T(8...) custom-call(s32[4]{0:T(128)} %pad_add_fusion.refs_0_, ...), custom_call_target="tpu_custom_call" | custom-call | flops 9663676416 | bytes 16515072 | tf_op jit(solution)/shard_map/pallas_call | solution.py:222
  276.3 8.3 %shard_map.228 = (bf16[4,272,1024]{2,1,0:T(8,128)(2,1)}, bf16[272,1024]{1,0:T(8,128)(2,1)}, bf16[272,1024]{1,0:T(8,128)(2,1)}, bf16[272,1024]{1,0:T(8,128)(2,1)}, bf16[272,1024]{1,0:T(8,128)(2,1)}) custom-call(s32[4]{0:T(128)} %pad_add_fusion.refs_0_, bf16[272,1024]{1,0:T(8,128)(2,1)} %get-tuple-element.131.refs_9_.refs_1_, ...), custom_call_target="tpu_custom_call" | custom-call | flops 2415919104 | bytes 4718592 | tf_op jit(solution)/shard_map/pallas_call | solution.py:222
  292.7 16.6 %shard_map.229 = (bf16[2,576,1024]{2,1,0:T(8,128)(2,1)}, bf16[2,576,1024]{2,1,0:T(8,128)(2,1)}, bf16[2,576,1024]{2,1,0:T(8,128)(2,1)}, bf16[2,576,512]{2,1,0:T(8...) custom-call(s32[4]{0:T(128)} %pad_add_fusion.refs_0_, ...), custom_call_target="tpu_custom_call" | custom-call | flops 9663676416 | bytes 16515072 | tf_op jit(solution)/shard_map/pallas_call | solution.py:222
  313.8 17.1 %shard_map.230 = (bf16[2,576,1024]{2,1,0:T(8,128)(2,1)}, bf16[2,576,1024]{2,1,0:T(8,128)(2,1)}, bf16[2,576,1024]{2,1,0:T(8,128)(2,1)}, bf16[2,576,512]{2,1,0:T(8...) custom-call(s32[4]{0:T(128)} %pad_add_fusion.refs_0_, ...), custom_call_target="tpu_custom_call" | custom-call | flops 9663676416 | bytes 16515072 | tf_op jit(solution)/shard_map/pallas_call | solution.py:222
  333.3 8.0 %shard_map.231 = (bf16[4,272,1024]{2,1,0:T(8,128)(2,1)}, bf16[272,1024]{1,0:T(8,128)(2,1)}, bf16[272,1024]{1,0:T(8,128)(2,1)}, bf16[272,1024]{1,0:T(8,128)(2,1)}, bf16[272,1024]{1,0:T(8,128)(2,1)}) custom-call(s32[4]{0:T(128)} %pad_add_fusion.refs_0_, bf16[272,1024]{1,0:T(8,128)(2,1)} %get-tuple-element.132.refs_9_.refs_1_, bf16[272,1024]{1,0:T(8,128)(2,1)} %copy-done.17, ...), custom_call_target="tpu_custom_call" | custom-call | flops 2415919104 | bytes 4718592 | tf_op jit(solution)/shard_map/pallas_call | solution.py:222
  348.1 13.4 %shard_map.232 = (bf16[2,256,1024]{2,1,0:T(8,128)(2,1)}, bf16[2,256,1024]{2,1,0:T(8,128)(2,1)}, bf16[2,256,1024]{2,1,0:T(8,128)(2,1)}, bf16[2,128,1024]{2,1,0:T(...) custom-call(bf16[2,576,1024]{2,1,0:T(8,128)(2,1)} %get-tuple-element, ...), custom_call_target="tpu_custom_call" | custom-call | flops 7247757312 | bytes 18874368 | tf_op jit(solution)/shard_map/pallas_call | solution.py:222
  364.7 13.4 %shard_map.233 = (bf16[2,256,1024]{2,1,0:T(8,128)(2,1)}, bf16[2,256,1024]{2,1,0:T(8,128)(2,1)}, bf16[2,256,1024]{2,1,0:T(8,128)(2,1)}, bf16[2,128,1024]{2,1,0:T(...) custom-call(bf16[2,576,1024]{2,1,0:T(8,128)(2,1)} %get-tuple-element, ...), custom_call_target="tpu_custom_call" | custom-call | flops 7247757312 | bytes 18874368 | tf_op jit(solution)/shard_map/pallas_call | solution.py:222
  384.3 9.0 %collective-permute-done.92 = bf16[2,512,256]{2,1,0:T(8,128)(2,1)S(1)} collective-permute-done((bf16[2,512,256]{2,1,0:T(8,128)(2,1)}, bf16[2,512,256]{2,1,0:T(8,128)(2,1)S(1)}, u32[]{:S(2)}, u32[]{:S(2)}) %collective-permute-start.92) | collective-permute-done | bytes 524320 | tf_op jit(solution)/shard_map/ppermute | solution.py:61
  399.5 4.9 shard_map.234
  404.5 9.4 %collective-permute-done.74 = bf16[2,256,1024]{2,1,0:T(8,128)(2,1)S(1)} collective-permute-done((bf16[2,256,1024]{2,1,0:T(8,128)(2,1)S(1)}, bf16[2,256,1024]{2,1,0:T(8,128)(2,1)S(1)}, u32[]{:S(2)}, u32[]{:S(2)}) %collective-permute-start.74) | collective-permute-done | bytes 1048608 | tf_op jit(solution)/shard_map/ppermute | solution.py:61
  423.0 8.5 %shard_map.235 = (bf16[256,1024]{1,0:T(8,128)(2,1)}, bf16[256,1024]{1,0:T(8,128)(2,1)}, bf16[256,1024]{1,0:T(8,128)(2,1)}, bf16[256,1024]{1,0:T(8,128)(2,1)}, bf16[256,1024]{1,0:T(8,128)(2,1)}) custom-call(s32[4]{0:T(128)} %pad_add_fusion.refs_0_, bf16[256,1024]{1,0:T(8,128)(2,1)} %get-tuple-element.324.refs_1_, ...), custom_call_target="tpu_custom_call" | custom-call | flops 5368709120 | bytes 8388608 | tf_op jit(solution)/shard_map/pallas_call | solution.py:222
  431.6 8.0 %shard_map.236 = (bf16[4,256,1024]{2,1,0:T(8,128)(2,1)}, bf16[256,1024]{1,0:T(8,128)(2,1)}, bf16[256,1024]{1,0:T(8,128)(2,1)}, bf16[256,1024]{1,0:T(8,128)(2,1)}, bf16[256,1024]{1,0:T(8,128)(2,1)}) custom-call(s32[4]{0:T(128)} %pad_add_fusion.refs_0_, bf16[272,1024]{1,0:T(8,128)(2,1)} %get-tuple-element.131.refs_9_.refs_1_, ...), custom_call_target="tpu_custom_call" | custom-call | flops 2415919104 | bytes 4718592 | tf_op jit(solution)/shard_map/pallas_call | solution.py:222
  448.9 11.2 %collective-permute-done.71 = bf16[272,1024]{1,0:T(8,128)(2,1)S(1)} collective-permute-done((bf16[272,1024]{1,0:T(8,128)(2,1)S(1)}, bf16[272,1024]{1,0:T(8,128)(2,1)S(1)}, u32[]{:S(2)}, u32[]{:S(2)}) %collective-permute-start.71) | collective-permute-done | bytes 557088 | tf_op jit(solution)/shard_map/ppermute | solution.py:157
  463.5 4.9 shard_map.237
  470.4 9.0 %shard_map.238 = (bf16[256,1024]{1,0:T(8,128)(2,1)}, bf16[256,1024]{1,0:T(8,128)(2,1)}, bf16[256,1024]{1,0:T(8,128)(2,1)}, bf16[256,1024]{1,0:T(8,128)(2,1)}, bf16[256,1024]{1,0:T(8,128)(2,1)}) custom-call(s32[4]{0:T(128)} %pad_add_fusion.refs_0_, bf16[256,1024]{1,0:T(8,128)(2,1)} %get-tuple-element.325.refs_1_, ...), custom_call_target="tpu_custom_call" | custom-call | flops 5368709120 | bytes 8388608 | tf_op jit(solution)/shard_map/pallas_call | solution.py:222
  482.3 8.0 %shard_map.239 = (bf16[4,256,1024]{2,1,0:T(8,128)(2,1)}, bf16[256,1024]{1,0:T(8,128)(2,1)}, bf16[256,1024]{1,0:T(8,128)(2,1)}, bf16[256,1024]{1,0:T(8,128)(2,1)}, bf16[256,1024]{1,0:T(8,128)(2,1)}) custom-call(s32[4]{0:T(128)} %pad_add_fusion.refs_0_, bf16[272,1024]{1,0:T(8,128)(2,1)} %get-tuple-element.132.refs_9_.refs_1_, bf16[272,1024]{1,0:T(8,128)(2,1)} %copy-done.17, ...), custom_call_target="tpu_custom_call" | custom-call | flops 2415919104 | bytes 4718592 | tf_op jit(solution)/shard_map/pallas_call | solution.py:222
  498.9 6.0 shard_map.240
  507.0 4.6 collective-permute-done.67
  513.9 14.5 %collective-permute-done.89.refs_9_ = bf16[256,1024]{1,0:T(8,128)(2,1)S(1)} collective-permute-done((bf16[256,1024]{1,0:T(8,128)(2,1)S(1)}, bf16[256,1024]{1,0:T(8,128)(2,1)S(1)}, u32[]{:S(2)}, u32[]{:S(2)}) %collective-permute-start.89) | collective-permute-done | bytes 524320 | tf_op jit(solution)/shard_map/ppermute | solution.py:1162
  529.2 6.0 shard_map.241
  536.1 4.1 convolution_convert_fusion
  565.2 9.9 %collective-permute-done.96 = bf16[2,128,1024]{2,1,0:T(8,128)(2,1)S(1)} collective-permute-done((bf16[2,128,1024]{2,1,0:T(8,128)(2,1)S(1)}, bf16[2,128,1024]{2,1,0:T(8,128)(2,1)S(1)}, u32[]{:S(2)}, u32[]{:S(2)}) %collective-permute-start.96) | collective-permute-done | bytes 524320 | tf_op jit(solution)/shard_map/ppermute | solution.py:61
  578.6 15.5 %collective-permute-done.94 = bf16[2,128,1024]{2,1,0:T(8,128)(2,1)S(1)} collective-permute-done((bf16[2,128,1024]{2,1,0:T(8,128)(2,1)S(1)}, bf16[2,128,1024]{2,1,0:T(8,128)(2,1)S(1)}, u32[]{:S(2)}, u32[]{:S(2)}) %collective-permute-start.94) | collective-permute-done | bytes 524320 | tf_op jit(solution)/shard_map/ppermute | solution.py:61
  606.6 12.1 %collective-permute-done.79 = bf16[256,1024]{1,0:T(8,128)(2,1)} collective-permute-done((bf16[256,1024]{1,0:T(8,128)(2,1)S(1)}, bf16[256,1024]{1,0:T(8,128)(2,1)}, u32[]{:S(2)}, u32[]{:S(2)}) %collective-permute-start.79) | collective-permute-done | bytes 524320 | tf_op jit(solution)/shard_map/ppermute | solution.py:157
  624.5 12.2 %collective-permute-done.81 = bf16[256,1024]{1,0:T(8,128)(2,1)S(1)} collective-permute-done((bf16[256,1024]{1,0:T(8,128)(2,1)S(1)}, bf16[256,1024]{1,0:T(8,128)(2,1)S(1)}, u32[]{:S(2)}, u32[]{:S(2)}) %collective-permute-start.81) | collective-permute-done | bytes 524320 | tf_op jit(solution)/shard_map/ppermute | solution.py:157
  638.8 9.1 %collective-permute-done.69 = bf16[256,1024]{1,0:T(8,128)(2,1)S(1)} collective-permute-done((bf16[256,1024]{1,0:T(8,128)(2,1)S(1)}, bf16[256,1024]{1,0:T(8,128)(2,1)S(1)}, u32[]{:S(2)}, u32[]{:S(2)}) %collective-permute-start.69) | collective-permute-done | bytes 524320 | tf_op jit(solution)/shard_map/ppermute | solution.py:157
  650.0 7.5 %collective-permute-done.83 = bf16[256,1024]{1,0:T(8,128)(2,1)} collective-permute-done((bf16[256,1024]{1,0:T(8,128)(2,1)}, bf16[256,1024]{1,0:T(8,128)(2,1)}, u32[]{:S(2)}, u32[]{:S(2)}) %collective-permute-start.83) | collective-permute-done | bytes 524320 | tf_op jit(solution)/shard_map/ppermute | solution.py:157
  660.5 32.5 %all-reduce.6.cloned.1.call-done = bf16[128,3200]{1,0:T(8,128)(2,1)} async-done(((bf16[128,3200]{1,0:T(8,128)(2,1)}), bf16[128,3200]{1,0:T(8,128)(2,1)}) %all-reduce.6.cloned.1.call-update) | async-done | bytes 819216 | tf_op jit(solution)/shard_map/psum | solution.py:1257
  (551 shorter events, 223.9 us)
Async XLA Ops:
  7.2 52.9 %all-gather.5.cloned.1.call-start = ((), (), s32[]{:S(2)}) async-start(), calls=%async_computation.3 | async-start | bytes 5308416 | tf_op jit(solution)/shard_map/all_gather | solution.py:982
  9.9 95.9 %all-gather.7.cloned.1.call-start = ((), (), s32[]{:S(2)}) async-start(), calls=%async_computation.4 | async-start | bytes 2654208 | tf_op jit(solution)/shard_map/all_gather | solution.py:983
  12.6 637.3 %reduce-scatter.2.cloned.1.call-start = ((), (), s32[]{:S(2)}) async-start(), calls=%async_computation.1 | async-start | bytes 7372800 | tf_op jit(solution)/shard_map/reduce_scatter | solution.py:1256
  20.4 41.0 %collective-permute-start.7 = (bf16[272,1024]{1,0:T(8,128)(2,1)}, bf16[272,1024]{1,0:T(8,128)(2,1)}, u32[]{:S(2)}, u32[]{:S(2)}) collective-permute-start(bf16[272,1024]{1,0:T(8,128)(2,1)} %get-tuple-element.131.refs_9_.refs_1_), channel_id=1, source_target_pairs={{0,4},{4,0},{8,12},{12,8},{16,20},{20,16},{24,28},{28,24},{1,5},{5... | collective-permute-start | bytes 1671176 | tf_op jit(solution)/shard_map/ppermute | solution.py:61
  20.4 27.6 %collective-permute-start.1 = (bf16[272,1024]{1,0:T(8,128)(2,1)}, bf16[272,1024]{1,0:T(8,128)(2,1)S(1)}, u32[]{:S(2)}, u32[]{:S(2)}) collective-permute-start(bf16[272,1024]{1,0:T(8,128)(2,1)} %get-tuple-element.132.refs_9_.refs_1_), channel_id=1, source_target_pairs={{0,1},{1,2},{2,3},{3,0},{4,5},{5,6},{6,7},{7,4},{8,9},{9,10},{10,1... | collective-permute-start | bytes 1671176 | tf_op jit(solution)/shard_map/ppermute | solution.py:157
  25.8 46.3 %collective-permute-start.19 = (bf16[4,128,1024]{2,1,0:T(8,128)(2,1)}, bf16[4,128,1024]{2,1,0:T(8,128)(2,1)}, u32[]{:S(2)}, u32[]{:S(2)}) collective-permute-start(bf16[4,128,1024]{2,1,0:T(8,128)(2,1)} %constant_dynamic-slice_fusion.1), channel_id=1, source_target_pairs={{0,4},{4,0},{8,12},{12,8},{16,20},{20,16},{24,28},{28,24},{1,5},{5... | collective-permute-start | bytes 3145736 | tf_op jit(solution)/shard_map/ppermute | solution.py:61
  36.2 23.9 %collective-permute-start.5 = (bf16[272,1024]{1,0:T(8,128)(2,1)}, bf16[272,1024]{1,0:T(8,128)(2,1)}, u32[]{:S(2)}, u32[]{:S(2)}) collective-permute-start(bf16[272,1024]{1,0:T(8,128)(2,1)} %collective-permute-done.refs_5_.refs_11_.refs_3_), channel_id=1, source_target_pairs={{0,1},{1,2},{2,3},{3,0},{4,5},{5,6},{6,7},{7,4},{8,9},{9,10},{10,1... | collective-permute-start | bytes 1671176 | tf_op jit(solution)/shard_map/ppermute | solution.py:157
  48.0 24.0 %collective-permute-start.6 = (bf16[272,1024]{1,0:T(8,128)(2,1)S(1)}, bf16[272,1024]{1,0:T(8,128)(2,1)}, u32[]{:S(2)}, u32[]{:S(2)}) collective-permute-start(bf16[272,1024]{1,0:T(8,128)(2,1)S(1)} %collective-permute-done.1.refs_6_.refs_11_.refs_3_), channel_id=1, source_target_pairs={{0,1},{1,2},{2,3},{3,0},{4,5},{5,6},{6,7},{7,4},{8,9},{9,10},{10,1... | collective-permute-start | bytes 1671176 | tf_op jit(solution)/shard_map/ppermute | solution.py:157
  50.5 33.4 %collective-permute-start.8 = (bf16[272,1024]{1,0:T(8,128)(2,1)}, bf16[272,1024]{1,0:T(8,128)(2,1)}, u32[]{:S(2)}, u32[]{:S(2)}) collective-permute-start(bf16[272,1024]{1,0:T(8,128)(2,1)} %collective-permute-done.refs_5_.refs_11_.refs_3_), channel_id=1, source_target_pairs={{0,4},{4,0},{8,12},{12,8},{16,20},{20,16},{24,28},{28,24},{1,5},{5... | collective-permute-start | bytes 1671176 | tf_op jit(solution)/shard_map/ppermute | solution.py:61
  61.4 26.2 %collective-permute-start.9 = (bf16[272,1024]{1,0:T(8,128)(2,1)}, bf16[272,1024]{1,0:T(8,128)(2,1)S(1)}, u32[]{:S(2)}, u32[]{:S(2)}) collective-permute-start(bf16[272,1024]{1,0:T(8,128)(2,1)} %collective-permute-done.5.refs_10_.refs_13_.refs_5_), channel_id=1, source_target_pairs={{0,4},{4,0},{8,12},{12,8},{16,20},{20,16},{24,28},{28,24},{1,5},{5... | collective-permute-start | bytes 1671176 | tf_op jit(solution)/shard_map/ppermute | solution.py:61
  72.0 24.4 %collective-permute-start.3 = (bf16[256,1024]{1,0:T(8,128)(2,1)}, bf16[256,1024]{1,0:T(8,128)(2,1)}, u32[]{:S(2)}, u32[]{:S(2)}) collective-permute-start(bf16[256,1024]{1,0:T(8,128)(2,1)} %get-tuple-element.134.refs_2_.refs_6_.refs_7_.refs_11_), channel_id=1, source_target_pairs={{0,8},{4,12},{1,9},{5,13},{2,10},{6,14},{3,11},{7,15},{16,24},{20,... | collective-permute-start | bytes 1572872 | tf_op jit(solution)/shard_map/ppermute | solution.py:1101
  94.9 42.4 %collective-permute-start.20 = (bf16[2,256,1024]{2,1,0:T(8,128)(2,1)}, bf16[2,256,1024]{2,1,0:T(8,128)(2,1)}, u32[]{:S(2)}, u32[]{:S(2)}) collective-permute-start(bf16[2,256,1024]{2,1,0:T(8,128)(2,1)} %get-tuple-element.139.refs_17_), channel_id=1, source_target_pairs={{0,8},{4,12},{8,0},{12,4},{16,24},{20,28},{24,16},{28,20},{1,9},{5... | collective-permute-start | bytes 3145736 | tf_op jit(solution)/shard_map/ppermute | solution.py:61
  99.8 53.7 %collective-permute-start.21 = (bf16[2,256,1024]{2,1,0:T(8,128)(2,1)}, bf16[2,256,1024]{2,1,0:T(8,128)(2,1)}, u32[]{:S(2)}, u32[]{:S(2)}) collective-permute-start(bf16[2,256,1024]{2,1,0:T(8,128)(2,1)} %get-tuple-element.139.refs_17_), channel_id=1, source_target_pairs={{0,16},{4,20},{8,24},{12,28},{16,0},{20,4},{24,8},{28,12},{1,17},{... | collective-permute-start | bytes 3145736 | tf_op jit(solution)/shard_map/ppermute | solution.py:61
  102.2 33.5 %collective-permute-start.34 = (bf16[256,1024]{1,0:T(8,128)(2,1)}, bf16[256,1024]{1,0:T(8,128)(2,1)S(1)}, u32[]{:S(2)}, u32[]{:S(2)}) collective-permute-start(bf16[256,1024]{1,0:T(8,128)(2,1)} %get-tuple-element.143.refs_2_.refs_6_.refs_7_.refs_11_), channel_id=1, source_target_pairs={{0,8},{4,12},{1,9},{5,13},{2,10},{6,14},{3,11},{7,15},{16,24},{20,... | collective-permute-start | bytes 1572872 | tf_op jit(solution)/shard_map/ppermute | solution.py:1101
  107.7 43.5 %collective-permute-start.26 = (bf16[2,512,256]{2,1,0:T(8,128)(2,1)}, bf16[2,512,256]{2,1,0:T(8,128)(2,1)S(1)}, u32[]{:S(2)}, u32[]{:S(2)}) collective-permute-start(bf16[2,512,256]{2,1,0:T(8,128)(2,1)} %get-tuple-element.140.refs_22_), channel_id=1, source_target_pairs={{0,16},{4,20},{8,24},{12,28},{16,0},{20,4},{24,8},{28,12},{1,17},{... | collective-permute-start | bytes 1572872 | tf_op jit(solution)/shard_map/ppermute | solution.py:61
  109.3 43.5 %collective-permute-start.33 = (bf16[256,1024]{1,0:T(8,128)(2,1)}, bf16[256,1024]{1,0:T(8,128)(2,1)S(1)}, u32[]{:S(2)}, u32[]{:S(2)}) collective-permute-start(bf16[256,1024]{1,0:T(8,128)(2,1)} %get-tuple-element.143.refs_2_.refs_6_.refs_7_.refs_11_), channel_id=1, source_target_pairs={{0,4},{8,12},{1,5},{9,13},{2,6},{10,14},{3,7},{11,15},{16,20},{24,... | collective-permute-start | bytes 1572872 | tf_op jit(solution)/shard_map/ppermute | solution.py:1100
  137.4 38.2 %collective-permute-start.35 = (bf16[256,1024]{1,0:T(8,128)(2,1)S(1)}, bf16[256,1024]{1,0:T(8,128)(2,1)S(1)}, u32[]{:S(2)}, u32[]{:S(2)}) collective-permute-start(bf16[256,1024]{1,0:T(8,128)(2,1)S(1)} %collective-permute-done.34.refs_4_.refs_8_.refs_9_.refs_13_), channel_id=1, source_target_pairs={{8,12},{12,8},{9,13},{13,9},{10,14},{14,10},{11,15},{15,11},{24,28... | collective-permute-start | bytes 1572872 | tf_op jit(solution)/shard_map/ppermute | solution.py:1102
  151.2 25.8 %collective-permute-start.22 = (bf16[2,128,1024]{2,1,0:T(8,128)(2,1)S(1)}, bf16[2,128,1024]{2,1,0:T(8,128)(2,1)}, u32[]{:S(2)}, u32[]{:S(2)}) collective-permute-start(bf16[2,128,1024]{2,1,0:T(8,128)(2,1)S(1)} %split.177.refs_10_), channel_id=1, source_target_pairs={{0,16},{4,20},{8,24},{12,28},{16,0},{20,4},{24,8},{28,12},{1,17},{... | collective-permute-start | bytes 1572872 | tf_op jit(solution)/shard_map/ppermute | solution.py:61
  157.1 33.6 %collective-permute-start.15 = (bf16[272,1024]{1,0:T(8,128)(2,1)}, bf16[272,1024]{1,0:T(8,128)(2,1)}, u32[]{:S(2)}, u32[]{:S(2)}) collective-permute-start(bf16[272,1024]{1,0:T(8,128)(2,1)} %collective-permute-done.13.refs_3_), channel_id=1, source_target_pairs={{0,1},{1,2},{2,3},{3,0},{4,5},{5,6},{6,7},{7,4},{8,9},{9,10},{10,1... | collective-permute-start | bytes 1671176 | tf_op jit(solution)/shard_map/ppermute | solution.py:157
  174.8 24.0 %collective-permute-start.31 = (bf16[2,512,256]{2,1,0:T(8,128)(2,1)S(1)}, bf16[2,512,256]{2,1,0:T(8,128)(2,1)S(1)}, u32[]{:S(2)}, u32[]{:S(2)}) collective-permute-start(bf16[2,512,256]{2,1,0:T(8,128)(2,1)S(1)} %copy-done.81), channel_id=1, source_target_pairs={{0,8},{4,12},{8,0},{12,4},{16,24},{20,28},{24,16},{28,20},{1,9},{5... | collective-permute-start | bytes 1572872 | tf_op jit(solution)/shard_map/ppermute | solution.py:61
  175.5 44.8 %collective-permute-start.29 = (bf16[2,256,1024]{2,1,0:T(8,128)(2,1)S(1)}, bf16[2,256,1024]{2,1,0:T(8,128)(2,1)S(1)}, u32[]{:S(2)}, u32[]{:S(2)}) collective-permute-start(bf16[2,256,1024]{2,1,0:T(8,128)(2,1)S(1)} %copy-done.51), channel_id=1, source_target_pairs={{0,8},{4,12},{8,0},{12,4},{16,24},{20,28},{24,16},{28,20},{1,9},{5... | collective-permute-start | bytes 3145736 | tf_op jit(solution)/shard_map/ppermute | solution.py:61
  177.0 44.8 %collective-permute-start.30 = (bf16[2,256,1024]{2,1,0:T(8,128)(2,1)S(1)}, bf16[2,256,1024]{2,1,0:T(8,128)(2,1)S(1)}, u32[]{:S(2)}, u32[]{:S(2)}) collective-permute-start(bf16[2,256,1024]{2,1,0:T(8,128)(2,1)S(1)} %copy-done.51), channel_id=1, source_target_pairs={{0,16},{4,20},{8,24},{12,28},{16,0},{20,4},{24,8},{28,12},{1,17},{... | collective-permute-start | bytes 3145736 | tf_op jit(solution)/shard_map/ppermute | solution.py:61
  190.8 31.1 %collective-permute-start.17 = (bf16[272,1024]{1,0:T(8,128)(2,1)}, bf16[272,1024]{1,0:T(8,128)(2,1)S(1)}, u32[]{:S(2)}, u32[]{:S(2)}) collective-permute-start(bf16[272,1024]{1,0:T(8,128)(2,1)} %collective-permute-done.15.refs_5_), channel_id=1, source_target_pairs={{0,1},{1,2},{2,3},{3,0},{4,5},{5,6},{6,7},{7,4},{8,9},{9,10},{10,1... | collective-permute-start | bytes 1671176 | tf_op jit(solution)/shard_map/ppermute | solution.py:157
  222.6 35.2 %collective-permute-start.41 = (bf16[2,256,256]{2,1,0:T(8,128)(2,1)S(1)}, bf16[2,256,256]{2,1,0:T(8,128)(2,1)}, u32[]{:S(2)}, u32[]{:S(2)}) collective-permute-start(bf16[2,256,256]{2,1,0:T(8,128)(2,1)S(1)} %split.183.refs_29_), channel_id=1, source_target_pairs={{0,16},{4,20},{8,24},{12,28},{16,0},{20,4},{24,8},{28,12},{1,17},{... | collective-permute-start | bytes 786440 | tf_op jit(solution)/shard_map/ppermute | solution.py:61
  224.1 33.7 %collective-permute-start.42 = (bf16[2,256,256]{2,1,0:T(8,128)(2,1)S(1)}, bf16[2,256,256]{2,1,0:T(8,128)(2,1)}, u32[]{:S(2)}, u32[]{:S(2)}) collective-permute-start(bf16[2,256,256]{2,1,0:T(8,128)(2,1)S(1)} %split.184.refs_30_), channel_id=1, source_target_pairs={{0,8},{4,12},{8,0},{12,4},{16,24},{20,28},{24,16},{28,20},{1,9},{5... | collective-permute-start | bytes 786440 | tf_op jit(solution)/shard_map/ppermute | solution.py:61
  257.8 27.4 %collective-permute-start.55 = (bf16[272,1024]{1,0:T(8,128)(2,1)S(1)}, bf16[272,1024]{1,0:T(8,128)(2,1)S(1)}, u32[]{:S(2)}, u32[]{:S(2)}) collective-permute-start(bf16[272,1024]{1,0:T(8,128)(2,1)S(1)} %copy-done.12), channel_id=1, source_target_pairs={{0,4},{4,0},{8,12},{12,8},{16,20},{20,16},{24,28},{28,24},{1,5},{5... | collective-permute-start | bytes 1671176 | tf_op jit(solution)/shard_map/ppermute | solution.py:61
  257.8 27.9 %collective-permute-start.56 = (bf16[272,1024]{1,0:T(8,128)(2,1)S(1)}, bf16[272,1024]{1,0:T(8,128)(2,1)S(1)}, u32[]{:S(2)}, u32[]{:S(2)}) collective-permute-start(bf16[272,1024]{1,0:T(8,128)(2,1)S(1)} %copy-done.14), channel_id=1, source_target_pairs={{0,4},{4,0},{8,12},{12,8},{16,20},{20,16},{24,28},{28,24},{1,5},{5... | collective-permute-start | bytes 1671176 | tf_op jit(solution)/shard_map/ppermute | solution.py:61
  258.3 27.6 %collective-permute-start.57 = (bf16[272,1024]{1,0:T(8,128)(2,1)}, bf16[272,1024]{1,0:T(8,128)(2,1)S(1)}, u32[]{:S(2)}, u32[]{:S(2)}) collective-permute-start(bf16[272,1024]{1,0:T(8,128)(2,1)} %collective-permute-done.6.refs_11_.refs_13_.refs_5_), channel_id=1, source_target_pairs={{0,4},{4,0},{8,12},{12,8},{16,20},{20,16},{24,28},{28,24},{1,5},{5... | collective-permute-start | bytes 1671176 | tf_op jit(solution)/shard_map/ppermute | solution.py:61
  288.6 43.6 %collective-permute-start.48 = (bf16[272,1024]{1,0:T(8,128)(2,1)}, bf16[272,1024]{1,0:T(8,128)(2,1)S(1)}, u32[]{:S(2)}, u32[]{:S(2)}) collective-permute-start(bf16[272,1024]{1,0:T(8,128)(2,1)} %get-tuple-element.155), channel_id=1, source_target_pairs={{0,4},{4,0},{8,12},{12,8},{16,20},{20,16},{24,28},{28,24},{1,5},{5... | collective-permute-start | bytes 1671176 | tf_op jit(solution)/shard_map/ppermute | solution.py:61
  382.7 31.1 %collective-permute-start.74 = (bf16[2,256,1024]{2,1,0:T(8,128)(2,1)S(1)}, bf16[2,256,1024]{2,1,0:T(8,128)(2,1)S(1)}, u32[]{:S(2)}, u32[]{:S(2)}) collective-permute-start(bf16[2,256,1024]{2,1,0:T(8,128)(2,1)S(1)} %copy-done.101), channel_id=1, source_target_pairs={{0,8},{4,12},{8,0},{12,4},{16,24},{20,28},{24,16},{28,20},{1,9},{5... | collective-permute-start | bytes 3145736 | tf_op jit(solution)/shard_map/ppermute | solution.py:61
  393.2 24.6 %collective-permute-start.75 = (bf16[2,256,1024]{2,1,0:T(8,128)(2,1)}, bf16[2,256,1024]{2,1,0:T(8,128)(2,1)S(1)}, u32[]{:S(2)}, u32[]{:S(2)}) collective-permute-start(bf16[2,256,1024]{2,1,0:T(8,128)(2,1)} %get-tuple-element.202), channel_id=1, source_target_pairs={{0,16},{4,20},{8,24},{12,28},{16,0},{20,4},{24,8},{28,12},{1,17},{... | collective-permute-start | bytes 3145736 | tf_op jit(solution)/shard_map/ppermute | solution.py:61
  396.2 24.5 %collective-permute-start.63 = (bf16[272,1024]{1,0:T(8,128)(2,1)}, bf16[272,1024]{1,0:T(8,128)(2,1)}, u32[]{:S(2)}, u32[]{:S(2)}) collective-permute-start(bf16[272,1024]{1,0:T(8,128)(2,1)} %get-tuple-element.188), channel_id=1, source_target_pairs={{0,4},{4,0},{8,12},{12,8},{16,20},{20,16},{24,28},{28,24},{1,5},{5... | collective-permute-start | bytes 1671176 | tf_op jit(solution)/shard_map/ppermute | solution.py:61
  398.1 50.2 %collective-permute-start.72 = (bf16[272,1024]{1,0:T(8,128)(2,1)}, bf16[272,1024]{1,0:T(8,128)(2,1)}, u32[]{:S(2)}, u32[]{:S(2)}) collective-permute-start(bf16[272,1024]{1,0:T(8,128)(2,1)} %get-tuple-element.196), channel_id=1, source_target_pairs={{0,4},{4,0},{8,12},{12,8},{16,20},{20,16},{24,28},{28,24},{1,5},{5... | collective-permute-start | bytes 1671176 | tf_op jit(solution)/shard_map/ppermute | solution.py:61
  413.9 27.8 %collective-permute-start.90 = (bf16[2,256,1024]{2,1,0:T(8,128)(2,1)S(1)}, bf16[2,256,1024]{2,1,0:T(8,128)(2,1)S(1)}, u32[]{:S(2)}, u32[]{:S(2)}) collective-permute-start(bf16[2,256,1024]{2,1,0:T(8,128)(2,1)S(1)} %copy-done.52), channel_id=1, source_target_pairs={{0,8},{4,12},{8,0},{12,4},{16,24},{20,28},{24,16},{28,20},{1,9},{5... | collective-permute-start | bytes 3145736 | tf_op jit(solution)/shard_map/ppermute | solution.py:61
  417.9 25.9 %collective-permute-start.91 = (bf16[2,256,1024]{2,1,0:T(8,128)(2,1)}, bf16[2,256,1024]{2,1,0:T(8,128)(2,1)S(1)}, u32[]{:S(2)}, u32[]{:S(2)}) collective-permute-start(bf16[2,256,1024]{2,1,0:T(8,128)(2,1)} %get-tuple-element.228), channel_id=1, source_target_pairs={{0,16},{4,20},{8,24},{12,28},{16,0},{20,4},{24,8},{28,12},{1,17},{... | collective-permute-start | bytes 3145736 | tf_op jit(solution)/shard_map/ppermute | solution.py:61
  445.0 62.0 %collective-permute-start.68 = (bf16[256,1024]{1,0:T(8,128)(2,1)}, bf16[256,1024]{1,0:T(8,128)(2,1)}, u32[]{:S(2)}, u32[]{:S(2)}) collective-permute-start(bf16[256,1024]{1,0:T(8,128)(2,1)} %get-tuple-element.193), channel_id=1, source_target_pairs={{0,4},{4,0},{8,12},{12,8},{16,20},{20,16},{24,28},{28,24},{1,5},{5... | collective-permute-start | bytes 1572872 | tf_op jit(solution)/shard_map/ppermute | solution.py:61
  445.0 34.4 %collective-permute-start.66 = (bf16[256,1024]{1,0:T(8,128)(2,1)}, bf16[256,1024]{1,0:T(8,128)(2,1)}, u32[]{:S(2)}, u32[]{:S(2)}) collective-permute-start(bf16[256,1024]{1,0:T(8,128)(2,1)} %get-tuple-element.192), channel_id=1, source_target_pairs={{0,4},{4,0},{8,12},{12,8},{16,20},{20,16},{24,28},{28,24},{1,5},{5... | collective-permute-start | bytes 1572872 | tf_op jit(solution)/shard_map/ppermute | solution.py:61
  446.8 49.3 %collective-permute-start.85 = (bf16[256,1024]{1,0:T(8,128)(2,1)}, bf16[256,1024]{1,0:T(8,128)(2,1)S(1)}, u32[]{:S(2)}, u32[]{:S(2)}) collective-permute-start(bf16[256,1024]{1,0:T(8,128)(2,1)} %get-tuple-element.218), channel_id=1, source_target_pairs={{4,0},{12,8},{5,1},{13,9},{6,2},{14,10},{7,3},{15,11},{20,16},{28,... | collective-permute-start | bytes 1572872 | tf_op jit(solution)/shard_map/ppermute | solution.py:1161
  448.3 31.8 %collective-permute-start.65 = (bf16[256,1024]{1,0:T(8,128)(2,1)S(1)}, bf16[256,1024]{1,0:T(8,128)(2,1)S(1)}, u32[]{:S(2)}, u32[]{:S(2)}) collective-permute-start(bf16[256,1024]{1,0:T(8,128)(2,1)S(1)} %fusion.45.refs_15_), channel_id=1, source_target_pairs={{0,1},{1,2},{2,3},{3,0},{4,5},{5,6},{6,7},{7,4},{8,9},{9,10},{10,1... | collective-permute-start | bytes 1572872 | tf_op jit(solution)/shard_map/ppermute | solution.py:157
  460.1 37.3 %collective-permute-start.86 = (bf16[256,1024]{1,0:T(8,128)(2,1)S(1)}, bf16[256,1024]{1,0:T(8,128)(2,1)S(1)}, u32[]{:S(2)}, u32[]{:S(2)}) collective-permute-start(bf16[256,1024]{1,0:T(8,128)(2,1)S(1)} %add_convert_fusion.6.refs_9_), channel_id=1, source_target_pairs={{8,0},{12,4},{9,1},{13,5},{10,2},{14,6},{11,3},{15,7},{24,16},{28,... | collective-permute-start | bytes 1572872 | tf_op jit(solution)/shard_map/ppermute | solution.py:1162
  497.4 31.0 %collective-permute-start.89 = (bf16[256,1024]{1,0:T(8,128)(2,1)S(1)}, bf16[256,1024]{1,0:T(8,128)(2,1)S(1)}, u32[]{:S(2)}, u32[]{:S(2)}) collective-permute-start(bf16[256,1024]{1,0:T(8,128)(2,1)S(1)} %add_convert_fusion.2.refs_11_), channel_id=1, source_target_pairs={{8,0},{12,4},{9,1},{13,5},{10,2},{14,6},{11,3},{15,7},{24,16},{28,... | collective-permute-start | bytes 1572872 | tf_op jit(solution)/shard_map/ppermute | solution.py:1162
  543.5 149.6 %all-reduce.6.cloned.1.call-start = ((), (), s32[]{:S(2)}) async-start(), calls=%async_computation.2 | async-start | bytes 1638400 | tf_op jit(solution)/shard_map/psum | solution.py:1257
  561.5 32.6 %collective-permute-start.94 = (bf16[2,128,1024]{2,1,0:T(8,128)(2,1)S(1)}, bf16[2,128,1024]{2,1,0:T(8,128)(2,1)S(1)}, u32[]{:S(2)}, u32[]{:S(2)}) collective-permute-start(bf16[2,128,1024]{2,1,0:T(8,128)(2,1)S(1)} %copy-done.26), channel_id=1, source_target_pairs={{0,16},{4,20},{8,24},{12,28},{16,0},{20,4},{24,8},{28,12},{1,17},{... | collective-permute-start | bytes 1572872 | tf_op jit(solution)/shard_map/ppermute | solution.py:61
  562.1 35.9 %collective-permute-start.95 = (bf16[2,128,1024]{2,1,0:T(8,128)(2,1)S(1)}, bf16[2,128,1024]{2,1,0:T(8,128)(2,1)S(1)}, u32[]{:S(2)}, u32[]{:S(2)}) collective-permute-start(bf16[2,128,1024]{2,1,0:T(8,128)(2,1)S(1)} %copy-done.27), channel_id=1, source_target_pairs={{0,8},{4,12},{8,0},{12,4},{16,24},{20,28},{24,16},{28,20},{1,9},{5... | collective-permute-start | bytes 1572872 | tf_op jit(solution)/shard_map/ppermute | solution.py:61
  565.2 37.7 %collective-permute-start.103 = (bf16[4,512,128]{2,1,0:T(8,128)(2,1)}, bf16[4,512,128]{2,1,0:T(8,128)(2,1)}, u32[]{:S(2)}, u32[]{:S(2)}) collective-permute-start(bf16[4,512,128]{2,1,0:T(8,128)(2,1)} %dynamic-slice_convert_fusion.1), channel_id=1, source_target_pairs={{0,4},{4,0},{8,12},{12,8},{16,20},{20,16},{24,28},{28,24},{1,5},{5... | collective-permute-start | bytes 1572872 | tf_op jit(solution)/shard_map/ppermute | solution.py:61
  602.9 35.9 %collective-permute-start.70 = (bf16[256,1024]{1,0:T(8,128)(2,1)}, bf16[256,1024]{1,0:T(8,128)(2,1)S(1)}, u32[]{:S(2)}, u32[]{:S(2)}) collective-permute-start(bf16[256,1024]{1,0:T(8,128)(2,1)} %get-tuple-element.194), channel_id=1, source_target_pairs={{0,4},{4,0},{8,12},{12,8},{16,20},{20,16},{24,28},{28,24},{1,5},{5... | collective-permute-start | bytes 1572872 | tf_op jit(solution)/shard_map/ppermute | solution.py:61
  606.0 43.9 %collective-permute-start.84 = (bf16[256,1024]{1,0:T(8,128)(2,1)}, bf16[256,1024]{1,0:T(8,128)(2,1)}, u32[]{:S(2)}, u32[]{:S(2)}) collective-permute-start(bf16[256,1024]{1,0:T(8,128)(2,1)} %get-tuple-element.215), channel_id=1, source_target_pairs={{0,4},{4,0},{8,12},{12,8},{16,20},{20,16},{24,28},{28,24},{1,5},{5... | collective-permute-start | bytes 1572872 | tf_op jit(solution)/shard_map/ppermute | solution.py:61
  621.9 26.0 %collective-permute-start.69 = (bf16[256,1024]{1,0:T(8,128)(2,1)S(1)}, bf16[256,1024]{1,0:T(8,128)(2,1)S(1)}, u32[]{:S(2)}, u32[]{:S(2)}) collective-permute-start(bf16[256,1024]{1,0:T(8,128)(2,1)S(1)} %copy-done.33), channel_id=1, source_target_pairs={{0,1},{1,2},{2,3},{3,0},{4,5},{5,6},{6,7},{7,4},{8,9},{9,10},{10,1... | collective-permute-start | bytes 1572872 | tf_op jit(solution)/shard_map/ppermute | solution.py:157
  (188 other events, 2483.8 us)
Sparse Core Ops, SparseCore 0:
  10.5 42.0 all-gather.4
  54.5 29.6 all-gather.6
  543.6 74.3 reduce-scatter.1
  650.1 42.9 all-reduce.5
